TPU v7x, 512 devices: a whole 4x4x16 slice. The times are simulated.
512 devices in a mesh: expert: 16 (over z), tensor: 32 (over y, x, core).
Axes of the slice: x: 4, y: 4, z: 16, core: 2. Of those that a mesh axis runs over, the one named last changes fastest.
Arguments:
- tokens: bfloat16 [512, 3072], P('expert', 'tensor'), may hold values from -6 to 6
- routes: int32 [512, 4], P('expert'), may hold values from 0 to 15, all different within a row; in each aligned block of 32 rows (0 to 31, 32 to 63, ...) at most 16 rows name the same one
- route_weight: int32 [512, 4], P('expert'), may hold values from 1 to 255
- w_gate: bfloat16 [16, 5376, 3072], P('expert', 'tensor'), may hold values from -0.109375 to 0.109375
- w_up: bfloat16 [16, 5376, 3072], P('expert', 'tensor'), may hold values from -0.109375 to 0.109375
- w_down: bfloat16 [16, 5376, 3072], P('expert', 'tensor'), may hold values from -0.078125 to 0.078125
Outputs:
- mixed: bfloat16 [512, 3072], P('expert', 'tensor')
Inputs may be any that keep to these rules, and one draw needn't show every extreme that they name: `routes`: within each aligned block of 32 rows the 4 experts of a row differ, no expert is named by more than 16 rows, a bound that some block reaches.
All inputs are finite; a program needn't handle non-finite values.
Results may differ from a plain program's by a relative error of at most 0.02.
Values may be sent and summed in bfloat16 or wider, within the bound.
No kernel may reach another device: no remote copies, remote signals or barrier semaphores. Data moves between devices by JAX's collectives and lax.ppermute only.
A program may use at most 64 MiB of HBM per device.

v0:
```python
import jax
import jax.numpy as jnp
from jax import lax
from jax.sharding import PartitionSpec as P


def slot_tables(routes, route_weight, experts, capacity):
    rows, top = routes.shape
    flat = routes.reshape(rows * top)
    marks = (flat[:, None] == jnp.arange(experts, dtype=jnp.int32)[None, :]).astype(jnp.int32)
    before = jnp.cumsum(marks, axis=0) - marks
    slot = jnp.sum(before * marks, axis=1)
    place = (flat * capacity + slot).reshape(rows, top)
    columns = jnp.arange(experts * capacity, dtype=jnp.int32)
    hits = (place[:, :, None] == columns[None, None, :]).astype(jnp.bfloat16)
    dispatch = jnp.sum(hits, axis=1)
    weight_f = route_weight.astype(jnp.float32)
    share = weight_f / jnp.sum(weight_f, axis=1, keepdims=True)
    return (dispatch, place, share)


def place_rows(dispatch, rows):
    placed = jnp.einsum("rs,rd->sd", dispatch, rows, preferred_element_type=jnp.float32)
    return placed.astype(jnp.bfloat16)


def times_rows(left, weight_rows):
    return lax.dot_general(
        left, weight_rows, (((1,), (1,)), ((), ())), preferred_element_type=jnp.float32
    )


def weighted_pick(returned, place, share):
    picked = jnp.take(returned, place, axis=0).astype(jnp.float32)
    return jnp.sum(picked * share[:, :, None], axis=1)


def local(tokens, routes, route_weight, w_gate, w_up, w_down):
    experts = lax.axis_size("expert")
    rows = tokens.shape[0]
    top = routes.shape[1]
    capacity = min(rows, 2 * rows * top // experts)
    dispatch, place, share = slot_tables(routes, route_weight, experts, capacity)
    gate_w = w_gate[0]
    up_w = w_up[0]
    down_w = w_down[0]
    whole = lax.all_gather(tokens, "tensor", axis=1, tiled=True)
    outgoing = place_rows(dispatch, whole).reshape(experts, capacity, whole.shape[1])
    arrived = lax.all_to_all(outgoing, "expert", split_axis=0, concat_axis=0, tiled=True)
    arrived = arrived.reshape(experts * capacity, whole.shape[1])
    gate = times_rows(arrived, gate_w)
    up = times_rows(arrived, up_w)
    hidden = (jax.nn.silu(gate) * up).astype(jnp.bfloat16)
    partial_value = jnp.dot(hidden, down_w, preferred_element_type=jnp.float32)
    summed = lax.psum_scatter(
        partial_value.astype(jnp.bfloat16), "tensor", scatter_dimension=1, tiled=True
    ).astype(jnp.float32)
    returned = lax.all_to_all(
        summed.reshape(experts, capacity, summed.shape[1]).astype(jnp.bfloat16),
        "expert",
        split_axis=0,
        concat_axis=0,
        tiled=True,
    ).astype(jnp.float32)
    returned = returned.reshape(experts * capacity, summed.shape[1])
    mixed = weighted_pick(returned, place, share)
    return mixed.astype(jnp.bfloat16)


def solution(mesh):
    placed = (
        P("expert", "tensor"),
        P("expert", None),
        P("expert", None),
        P("expert", "tensor", None),
        P("expert", "tensor", None),
        P("expert", "tensor", None),
    )
    return jax.shard_map(
        local, mesh=mesh, in_specs=placed, out_specs=P("expert", "tensor"), check_vma=False
    )
```

profile of v0, /device:TPU:2, one launch (start us, length us, event | category | flops | bytes accessed | tf_op | source)
XLA Modules:
  0.0 259.2 jit_solution(11211405290988885193)
XLA Ops:
  6.5 0.0 copy-start
  6.5 0.0 reduce-scatter.2.cloned.1.call-start
  6.5 0.8 copy.31
  7.4 0.1 eq.28
  7.5 0.1 fusion.14
  7.6 0.2 reduce_window_sum.11
  7.8 0.2 select_reduce_fusion
  7.9 0.1 reduce_sum.42
  8.1 0.1 copy.32
  8.1 0.7 compare_and_fusion
  8.8 0.1 fusion.13
  8.9 27.6 %all-gather = bf16[32,96,32]{1,2,0:T(8,128)(2,1)S(1)} all-gather(bf16[1,96,32]{1,2,0:T(8,128)(2,1)} %bitcast.30), channel_id=1, replica_groups=mesh['expert'=16,'tensor'=32] {'tensor'}, dimensions={0}, use_global_device_ids=true | all-gather | bytes 202752 | tf_op jit(solution)/shard_map/all_gather | solution.py:47
  36.6 0.1 copy.34
  36.7 0.3 reshape.48
  37.0 0.6 convolution_convert_fusion
  37.6 0.0 copy-start.1
  37.6 86.8 %all_to_all.10 = bf16[16,16,3072]{2,1,0:T(8,128)(2,1)S(1)} all-to-all(bf16[16,16,3072]{2,1,0:T(8,128)(2,1)S(1)} %bitcast.28), channel_id=1, replica_groups=mesh['expert'=16,'tensor'=32] {'expert'}, dimensions={0} | all-to-all | bytes 3145728 | tf_op jit(solution)/shard_map/all_to_all | solution.py:49
  124.4 0.0 copy-done.1
  124.4 0.7 fusion.4
  125.1 0.0 copy-done
  125.1 4.3 %convolution_convert_fusion.1 = bf16[256,3072]{0,1:T(8,128)(2,1)} fusion(bf16[256,3072]{1,0:T(8,128)(2,1)S(1)} %bitcast.27, bf16[1,168,3072]{2,1,0:T(8,128)(2,1)S(1)} %copy-done, bf16[1,168,3072]{2,1,0:T(8,128)(2,1)} %param.10, f32[256,168]{0,1:T(8,128)S(1)} %fusion.4), kind=kOutput, calls=%fused_computation.2 | convolution fusion | flops 529526784 | bytes 5382144 | tf_op jit(solution)/shard_map/dot_general | solution.py:54
  129.4 0.0 copy-start.2
  129.4 0.0 reduce-scatter.2.cloned.1.call-update
  129.4 0.7 copy-done.2
  130.1 94.2 %reduce-scatter.2.cloned.1.call-done = bf16[256,96]{0,1:T(8,128)(2,1)} async-done(((bf16[256,3072]{0,1:T(8,128)(2,1)}), bf16[256,96]{0,1:T(8,128)(2,1)}) %reduce-scatter.2.cloned.1.call-update) | async-done | bytes 49168 | tf_op jit(solution)/shard_map/reduce_scatter | solution.py:55
  224.3 1.5 copy.35
  225.8 12.2 %all-to-all-start.1 = ((bf16[16,16,96]{2,1,0:T(8,128)(2,1)}), bf16[16,16,96]{2,1,0:T(8,128)(2,1)S(1)}, u32[]{:S(2)}, u32[]{:S(2)}) async-start(bf16[16,16,96]{2,1,0:T(8,128)(2,1)} %bitcast.7), calls=%async_computation.2 | async-start | bytes 131072 | tf_op jit(solution)/shard_map/all_to_all | solution.py:58
  238.1 0.1 copy.36
  238.2 0.1 reshape.39
  238.3 0.1 copy.33
  238.4 0.1 copy.37
  238.5 12.5 %all-to-all-done.1 = bf16[16,16,96]{2,1,0:T(8,128)(2,1)S(1)} async-done(((bf16[16,16,96]{2,1,0:T(8,128)(2,1)}), bf16[16,16,96]{2,1,0:T(8,128)(2,1)S(1)}, u32[]{:S(2)}, u32[]{:S(2)}) %all-to-all-start.1) | async-done | bytes 49184 | tf_op jit(solution)/shard_map/all_to_all | solution.py:58
  251.0 0.6 gather_fusion
  251.6 0.8 multiply_reduce_fusion
  (5 shorter events, 0.1 us)
Async XLA Ops:
  6.5 118.5 %copy-start = (bf16[1,168,3072]{2,1,0:T(8,128)(2,1)S(1)}, bf16[1,168,3072]{2,1,0:T(8,128)(2,1)}, u32[]{:S(2)}) copy-start(bf16[1,168,3072]{2,1,0:T(8,128)(2,1)} %param.11) | copy-start | bytes 3096580
  6.5 217.8 %reduce-scatter.2.cloned.1.call-start = ((), (), s32[]{:S(2)}) async-start(), calls=%async_computation.3 | async-start | bytes 1622016 | tf_op jit(solution)/shard_map/reduce_scatter | solution.py:55
  37.6 86.8 %copy-start.1 = (bf16[1,168,3072]{2,1,0:T(8,128)(2,1)S(1)}, bf16[1,168,3072]{2,1,0:T(8,128)(2,1)}, u32[]{:S(2)}) copy-start(bf16[1,168,3072]{2,1,0:T(8,128)(2,1)} %param.9) | copy-start | bytes 3096580
  129.4 0.7 copy-start.2
  225.8 25.1 %all-to-all-start.1 = ((bf16[16,16,96]{2,1,0:T(8,128)(2,1)}), bf16[16,16,96]{2,1,0:T(8,128)(2,1)S(1)}, u32[]{:S(2)}, u32[]{:S(2)}) async-start(bf16[16,16,96]{2,1,0:T(8,128)(2,1)} %bitcast.7), calls=%async_computation.2 | async-start | bytes 131072 | tf_op jit(solution)/shard_map/all_to_all | solution.py:58
Sparse Core Ops, SparseCore 0:
  129.6 94.6 reduce-scatter.1
where the time goes:
time: 260 us; the launch traced here: 259 us
  blocking collectives  114 us (44%)
  waiting for transfers between devices  107 us (41%)
  between operations  13.5 us (5%)
  starting transfers between devices  12.3 us (5%)
  matrix products  5.58 us (2%)
  local copies, waits for them, and re-layouts  4.79 us (2%)
    reduce_scatter x1, waiting for transfers between devices, local(): lax.psum_scatter(partial_value.astype(jnp.bfloat16), 'tensor', scatter_di...  94.2 us
    all_to_all x1, blocking collectives, local(): lax.all_to_all(outgoing, 'expert', split_axis=0, concat_axis=0, tiled=True)  86.8 us
    all_gather x1, blocking collectives, local(): whole = lax.all_gather(tokens, 'tensor', axis=1, tiled=True)  27.6 us
    all_to_all x1, waiting for transfers between devices, local(): lax.all_to_all(summed.reshape(experts, capacity, summed.shape[1]).astype(...  12.5 us
    all_to_all x1, starting transfers between devices, local(): lax.all_to_all(summed.reshape(experts, capacity, summed.shape[1]).astype(...  12.2 us
  transfers between devices with their start and end apart: 2, of which 2 were waited for; matrix products, arithmetic and copies ran while one was open for 0% of the time, Pallas kernels for 0%

commit v1 on v0

v1 whole, which is shorter than its diff:
```python
import functools

import jax
import jax.numpy as jnp
from jax import lax
from jax.experimental import pallas as pl
from jax.experimental.pallas import tpu as pltpu
from jax.sharding import Mesh, PartitionSpec as P

GRID = ("y", "x")
VMEM = pl.BlockSpec(memory_space=pltpu.VMEM)
BF16 = jnp.bfloat16
F32 = jnp.float32


def dot(left, right, dims, precision=None):
    return lax.dot_general(left, right, (dims, ((), ())), precision=precision, preferred_element_type=F32)


def eye(n):
    same = lax.broadcasted_iota(jnp.int32, (n, n), 0) == lax.broadcasted_iota(jnp.int32, (n, n), 1)
    return same.astype(F32).astype(BF16)


def call(body, out, operands, scratch=(), flops=0, moved=0):
    return pl.pallas_call(
        body,
        out_shape=out,
        in_specs=[VMEM] * len(operands),
        out_specs=jax.tree.map(lambda _: VMEM, out),
        scratch_shapes=list(scratch),
        compiler_params=pltpu.CompilerParams(vmem_limit_bytes=40 * 2**20),
        cost_estimate=pl.CostEstimate(flops=flops, bytes_accessed=moved, transcendentals=0),
    )(*operands)


def place_kernel(capacity, tokens_ref, routes_ref, weight_ref, placed_ref, mix_ref):
    rows, top = routes_ref.shape
    columns = placed_ref.shape[0]
    column = lax.broadcasted_iota(jnp.int32, (rows, columns), 1)
    expert = column // capacity
    spot = column % capacity
    weight = weight_ref[...].astype(F32)
    share = weight / jnp.sum(weight, axis=1, keepdims=True)
    named = jnp.zeros((rows, columns), F32)
    mix = jnp.zeros((rows, columns), F32)
    for k in range(top):
        hit = routes_ref[:, k : k + 1] == expert
        named += jnp.where(hit, 1.0, 0.0)
        mix += jnp.where(hit, share[:, k : k + 1], 0.0)
    earlier = lax.broadcasted_iota(jnp.int32, (rows, rows), 1) < lax.broadcasted_iota(jnp.int32, (rows, rows), 0)
    before = dot(earlier.astype(F32).astype(BF16), named.astype(BF16), ((1,), (0,)))
    here = (named > 0.5) & (before.astype(jnp.int32) == spot)
    mix_ref[...] = jnp.where(here, mix, 0.0)
    dispatch = jnp.where(here, 1.0, 0.0).astype(BF16)
    placed_ref[...] = dot(dispatch, tokens_ref[...], ((0,), (0,))).astype(BF16)


def turn_kernel(arrived_ref, copies_ref):
    n, depth, _ = copies_ref.shape
    turned = dot(eye(depth), arrived_ref[...], ((1,), (1,))).astype(BF16)
    for i in range(n):
        copies_ref[i] = turned


def expert_kernel(own_ref, other_ref, core_ref, gate_ref, up_ref, down_ref, keep_ref, send_ref, x_ref, part_ref):
    n, depth, _ = own_ref.shape
    core = core_ref[0]

    def rows(i, which):
        return pl.ds(pl.multiple_of((2 * i + which) * depth, depth), depth)

    for i in range(n):
        x_ref[rows(i, core)] = own_ref[i]
        x_ref[rows(i, 1 - core)] = other_ref[i]
    gate = dot(gate_ref[...], x_ref[...], ((1,), (0,)))
    up = dot(up_ref[...], x_ref[...], ((1,), (0,)))
    hidden = (gate / (1.0 + jnp.exp(-gate)) * up).astype(BF16)
    part_ref[...] = dot(down_ref[...], hidden, ((0,), (0,))).astype(BF16)
    for i in range(n):
        keep_ref[i] = part_ref[rows(i, core)]
        send_ref[i] = part_ref[rows(i, 1 - core)]


def pair_kernel(keep_ref, got_ref, out_ref):
    out_ref[...] = (keep_ref[...].astype(F32) + got_ref[...].astype(F32)).astype(BF16)


def sum_kernel(pieces_ref, out_ref):
    n, depth, _ = pieces_ref.shape
    total = pieces_ref[0].astype(F32)
    for i in range(1, n):
        total += pieces_ref[i].astype(F32)
    out_ref[...] = dot(total.astype(BF16), eye(depth), ((0,), (0,))).astype(BF16)


def mix_kernel(mix_ref, returned_ref, out_ref):
    rest = mix_ref[...]
    values = returned_ref[...]
    total = jnp.zeros(out_ref.shape, F32)
    for _ in range(3):
        piece = rest.astype(BF16)
        rest = rest - piece.astype(F32)
        total += dot(piece, values, ((1,), (0,)))
    out_ref[...] = total.astype(BF16)


def local(tokens, routes, route_weight, w_gate, w_up, w_down):
    experts, chips = lax.axis_size("expert"), lax.axis_size(GRID)
    rows, depth = tokens.shape
    capacity = min(rows, 2 * rows * routes.shape[1] // experts)
    slots = experts * capacity
    shape = jax.ShapeDtypeStruct
    swap = functools.partial(lax.ppermute, axis_name="core", perm=((0, 1), (1, 0)))

    placed, mix = call(
        functools.partial(place_kernel, capacity),
        (shape((slots, depth), BF16), shape((rows, slots), F32)),
        (tokens, routes, route_weight),
    )
    arrived = lax.all_to_all(placed.reshape(experts, capacity, depth), "expert", 0, 0, tiled=True)
    copies = call(turn_kernel, shape((chips, depth, slots), BF16), (arrived.reshape(slots, depth),))
    own = lax.all_to_all(copies, GRID, 0, 0, tiled=True)
    other = swap(own)
    core = lax.axis_index("core").astype(jnp.int32).reshape(1)
    operands = (own, other, core, w_gate[0], w_up[0], w_down[0])
    whole = 2 * chips * depth
    half = shape((chips, depth, slots), BF16)
    keep, send = pl.pallas_call(
        expert_kernel,
        out_shape=(half, half),
        in_specs=[VMEM, VMEM, pl.BlockSpec(memory_space=pltpu.SMEM), VMEM, VMEM, VMEM],
        out_specs=(VMEM, VMEM),
        scratch_shapes=[pltpu.VMEM((whole, slots), BF16), pltpu.VMEM((whole, slots), BF16)],
        compiler_params=pltpu.CompilerParams(vmem_limit_bytes=40 * 2**20),
    )(*operands)
    got = swap(send)
    paired = call(pair_kernel, half, (keep, got))
    pieces = lax.all_to_all(paired, GRID, 0, 0, tiled=True)
    summed = call(sum_kernel, shape((slots, depth), BF16), (pieces,))
    returned = lax.all_to_all(summed.reshape(experts, capacity, depth), "expert", 0, 0, tiled=True)
    return call(mix_kernel, shape((rows, depth), BF16), (mix, returned.reshape(slots, depth)))


def solution(mesh):
    chips_y = chips_x = 4
    devices = mesh.devices
    fine = Mesh(devices.reshape(devices.shape[0], chips_y, chips_x, 2), ("expert", "y", "x", "core"))
    tensor = ("y", "x", "core")
    placed = (
        P("expert", tensor),
        P("expert", None),
        P("expert", None),
        P("expert", tensor, None),
        P("expert", tensor, None),
        P("expert", tensor, None),
    )
    return jax.shard_map(local, mesh=fine, in_specs=placed, out_specs=P("expert", tensor), check_vma=False)
```

time: 260 us -> 96.6 us (0.37)
  waiting for transfers between devices: 107 us -> 4.51 us
  blocking collectives: 114 us -> 80.4 us
  between operations: 13.5 us -> 0.06 us
  starting transfers between devices: 12.3 us -> 3.95 us
  matrix products: 5.58 us -> 0 us
  Pallas kernels: 0 us -> 4.52 us
    reduce_scatter x1 -> x0, waiting for transfers between devices: 94.2 us -> none  [local(): lax.psum_scatter(partial_value.astype(jnp.bfloat16), 'tensor', scatter_di...]
    all_gather x1 -> x0, blocking collectives: 27.6 us -> none  [local(): whole = lax.all_gather(tokens, 'tensor', axis=1, tiled=True)]
    all_to_all x1 -> x0, waiting for transfers between devices: 12.5 us -> none  [local(): lax.all_to_all(summed.reshape(experts, capacity, summed.shape[1]).astype(...]
    all_to_all x1 -> x0, starting transfers between devices: 12.2 us -> none  [local(): lax.all_to_all(summed.reshape(experts, capacity, summed.shape[1]).astype(...]
    all_to_all x1 -> x4, blocking collectives: 86.8 us -> 80.4 us  [the longest x1 27.7 us: local(): lax.all_to_all(placed.reshape(experts, capacity, depth), 'expert', 0, 0,...]
    dot_general x3 -> x0, matrix products: 5.58 us -> none  [the longest x1 4.32 us: local(): partial_value = jnp.dot(hidden, down_w, preferred_element_type=jnp.float32)]
    pallas_call x0 -> x6, Pallas kernels: none -> 4.52 us  [the longest x1 2.65 us: local(): pl.pallas_call(expert_kernel, out_shape=(half, half), in_specs=[VMEM, VME...]
    ppermute x0 -> x2, waiting for transfers between devices: none -> 4.51 us  [the longest x1 2.38 us: local(): other = swap(own)]
where the time goes in v1:
time: 96.6 us; the launch traced here: 96.1 us
  blocking collectives  80.4 us (83%)
  Pallas kernels  4.52 us (5%)
  waiting for transfers between devices  4.51 us (5%)
  starting transfers between devices  3.95 us (4%)
  local copies, waits for them, and re-layouts  2.7 us (3%)
    all_to_all x1, blocking collectives, local(): lax.all_to_all(placed.reshape(experts, capacity, depth), 'expert', 0, 0,...  27.7 us
    all_to_all x1, blocking collectives, local(): own = lax.all_to_all(copies, GRID, 0, 0, tiled=True)  19 us
    all_to_all x1, blocking collectives, local(): pieces = lax.all_to_all(paired, GRID, 0, 0, tiled=True)  17.5 us
    all_to_all x1, blocking collectives, local(): lax.all_to_all(summed.reshape(experts, capacity, depth), 'expert', 0, 0,...  16.1 us
    unnamed x12, local copies, waits for them, and re-layouts  2.7 us
    pallas_call x1, Pallas kernels, local(): pl.pallas_call(expert_kernel, out_shape=(half, half), in_specs=[VMEM, VME...  2.65 us
    ppermute x1, waiting for transfers between devices, local(): other = swap(own)  2.38 us
    ppermute x1, waiting for transfers between devices, local(): got = swap(send)  2.13 us
  transfers between devices with their start and end apart: 2, of which 2 were waited for; matrix products, arithmetic and copies ran while one was open for 0% of the time, Pallas kernels for 0%

profile of v1, /device:TPU:2, one launch (start us, length us, event | category | flops | bytes accessed | tf_op | source)
XLA Modules:
  0.0 96.1 jit_solution(7576656153988955342)
XLA Ops:
  0.0 0.0 copy-start.4
  0.0 0.8 copy.7.routes_ref
  0.8 0.0 copy-done.4
  0.8 0.0 copy-start.3
  0.8 0.1 copy.8.weight_ref
  0.9 0.6 copy-done.3
  1.5 0.4 shard_map.64
  1.9 27.7 %all_to_all.20 = bf16[16,16,96]{2,1,0:T(8,128)(2,1)S(1)} all-to-all(bf16[16,16,96]{2,1,0:T(8,128)(2,1)S(1)} %bitcast.14), channel_id=1, replica_groups=mesh['expert'=16,'y'=4,'x'=4,'core'=2] {'expert'}, dimensions={0} | all-to-all | bytes 98304 | tf_op jit(solution)/shard_map/all_to_all | solution.py:121
  29.6 0.0 copy-start
  29.6 0.0 copy-start.1
  29.6 0.2 shard_map.65
  29.9 19.0 %all_to_all.21.own_ref = bf16[16,96,256]{2,1,0:T(8,128)(2,1)S(1)} all-to-all(bf16[16,96,256]{2,1,0:T(8,128)(2,1)S(1)} %shard_map.65), channel_id=1, replica_groups=mesh['expert'=16,'y'=4,'x'=4,'core'=2] {'y','x'}, dimensions={0} | all-to-all | bytes 1572864 | tf_op jit(solution)/shard_map/all_to_all | solution.py:123
  48.9 1.9 %collective-permute-start = (bf16[16,96,256]{2,1,0:T(8,128)(2,1)S(1)}, bf16[16,96,256]{2,1,0:T(8,128)(2,1)}, u32[]{:S(2)}, u32[]{:S(2)}) collective-permute-start(bf16[16,96,256]{2,1,0:T(8,128)(2,1)S(1)} %all_to_all.21.own_ref), channel_id=1, source_target_pairs={{0,1},{1,0},{2,3},{3,2},{4,5},{5,4},{6,7},{7,6},{8,9},{9,8},{10,11... | collective-permute-start | bytes 2359304 | tf_op jit(solution)/shard_map/ppermute | solution.py:124
  50.8 2.4 %collective-permute-done.other_ref = bf16[16,96,256]{2,1,0:T(8,128)(2,1)} collective-permute-done((bf16[16,96,256]{2,1,0:T(8,128)(2,1)S(1)}, bf16[16,96,256]{2,1,0:T(8,128)(2,1)}, u32[]{:S(2)}, u32[]{:S(2)}) %collective-permute-start) | collective-permute-done | bytes 786464 | tf_op jit(solution)/shard_map/ppermute | solution.py:124
  53.2 0.0 copy-done
  53.2 0.0 copy-done.1
  53.2 0.0 copy-start.2
  53.2 1.2 %copy-done.2 = bf16[1,168,3072]{2,1,0:T(8,128)(2,1)S(1)} copy-done((bf16[1,168,3072]{2,1,0:T(8,128)(2,1)S(1)}, bf16[1,168,3072]{2,1,0:T(8,128)(2,1)}, u32[]{:S(2)}) %copy-start.2) | copy-done | bytes 1032216
  54.4 2.6 %shard_map.66 = (bf16[16,96,256]{2,1,0:T(8,128)(2,1)S(1)}, bf16[16,96,256]{2,1,0:T(8,128)(2,1)S(1)}) custom-call(bf16[16,96,256]{2,1,0:T(8,128)(2,1)S(1)} %all_to_all.21.own_ref, bf16[16,96,256]{2,1,0:T(8,128)(2,1)} %collective-permute-done.other_ref, s32[1]{0:T(128)} %bitcast.2.core_ref, bf16[168,3072]{1,0:T(8,128)(2,1)S(1)} %bitcast.8, ...), custom_call_target="tpu_custom_call" | custom-call | tf_op jit(solution)/shard_map/pallas_call | solution.py:129
  57.0 2.0 %collective-permute-start.1 = (bf16[16,96,256]{2,1,0:T(8,128)(2,1)S(1)}, bf16[16,96,256]{2,1,0:T(8,128)(2,1)S(1)}, u32[]{:S(2)}, u32[]{:S(2)}) collective-permute-start(bf16[16,96,256]{2,1,0:T(8,128)(2,1)S(1)} %get-tuple-element.12), channel_id=1, source_target_pairs={{0,1},{1,0},{2,3},{3,2},{4,5},{5,4},{6,7},{7,6},{8,9},{9,8},{10,11... | collective-permute-start | bytes 2359304 | tf_op jit(solution)/shard_map/ppermute | solution.py:137
  59.1 2.1 %collective-permute-done.1.got_ref = bf16[16,96,256]{2,1,0:T(8,128)(2,1)S(1)} collective-permute-done((bf16[16,96,256]{2,1,0:T(8,128)(2,1)S(1)}, bf16[16,96,256]{2,1,0:T(8,128)(2,1)S(1)}, u32[]{:S(2)}, u32[]{:S(2)}) %collective-permute-start.1) | collective-permute-done | bytes 786464 | tf_op jit(solution)/shard_map/ppermute | solution.py:137
  61.2 0.2 shard_map.67
  61.4 17.5 %all_to_all.22.pieces_ref = bf16[16,96,256]{2,1,0:T(8,128)(2,1)S(1)} all-to-all(bf16[16,96,256]{2,1,0:T(8,128)(2,1)S(1)} %shard_map.67), channel_id=1, replica_groups=mesh['expert'=16,'y'=4,'x'=4,'core'=2] {'y','x'}, dimensions={0} | all-to-all | bytes 1572864 | tf_op jit(solution)/shard_map/all_to_all | solution.py:139
  78.9 0.3 shard_map.68
  79.2 16.1 %all_to_all.23 = bf16[16,16,96]{2,1,0:T(8,128)(2,1)S(1)} all-to-all(bf16[16,16,96]{2,1,0:T(8,128)(2,1)S(1)} %bitcast.13), channel_id=1, replica_groups=mesh['expert'=16,'y'=4,'x'=4,'core'=2] {'expert'}, dimensions={0} | all-to-all | bytes 98304 | tf_op jit(solution)/shard_map/all_to_all | solution.py:141
  95.4 0.8 shard_map.69
Async XLA Ops:
  0.0 0.8 copy-start.4
  0.8 0.7 copy-start.3
  29.6 23.5 %copy-start = (bf16[1,168,3072]{2,1,0:T(8,128)(2,1)S(1)}, bf16[1,168,3072]{2,1,0:T(8,128)(2,1)}, u32[]{:S(2)}) copy-start(bf16[1,168,3072]{2,1,0:T(8,128)(2,1)} %param.9) | copy-start | bytes 3096580
  29.6 23.5 %copy-start.1 = (bf16[1,168,3072]{2,1,0:T(8,128)(2,1)S(1)}, bf16[1,168,3072]{2,1,0:T(8,128)(2,1)}, u32[]{:S(2)}) copy-start(bf16[1,168,3072]{2,1,0:T(8,128)(2,1)} %param.10) | copy-start | bytes 3096580
  48.9 4.3 %collective-permute-start = (bf16[16,96,256]{2,1,0:T(8,128)(2,1)S(1)}, bf16[16,96,256]{2,1,0:T(8,128)(2,1)}, u32[]{:S(2)}, u32[]{:S(2)}) collective-permute-start(bf16[16,96,256]{2,1,0:T(8,128)(2,1)S(1)} %all_to_all.21.own_ref), channel_id=1, source_target_pairs={{0,1},{1,0},{2,3},{3,2},{4,5},{5,4},{6,7},{7,6},{8,9},{9,8},{10,11... | collective-permute-start | bytes 2359304 | tf_op jit(solution)/shard_map/ppermute | solution.py:124
  53.2 1.2 %copy-start.2 = (bf16[1,168,3072]{2,1,0:T(8,128)(2,1)S(1)}, bf16[1,168,3072]{2,1,0:T(8,128)(2,1)}, u32[]{:S(2)}) copy-start(bf16[1,168,3072]{2,1,0:T(8,128)(2,1)} %param.11) | copy-start | bytes 3096580
  57.0 4.2 %collective-permute-start.1 = (bf16[16,96,256]{2,1,0:T(8,128)(2,1)S(1)}, bf16[16,96,256]{2,1,0:T(8,128)(2,1)S(1)}, u32[]{:S(2)}, u32[]{:S(2)}) collective-permute-start(bf16[16,96,256]{2,1,0:T(8,128)(2,1)S(1)} %get-tuple-element.12), channel_id=1, source_target_pairs={{0,1},{1,0},{2,3},{3,2},{4,5},{5,4},{6,7},{7,6},{8,9},{9,8},{10,11... | collective-permute-start | bytes 2359304 | tf_op jit(solution)/shard_map/ppermute | solution.py:137

commit v2 on v1

v2 whole, which is shorter than its diff:
```python
import functools
import math

import jax
import jax.numpy as jnp
from jax import lax
from jax.experimental import pallas as pl
from jax.experimental.pallas import tpu as pltpu
from jax.sharding import Mesh, PartitionSpec as P

GRID = ("y", "x")
VMEM = pl.BlockSpec(memory_space=pltpu.VMEM)
BF16 = jnp.bfloat16
F32 = jnp.float32


def dot(left, right, dims, precision=None):
    return lax.dot_general(left, right, (dims, ((), ())), precision=precision, preferred_element_type=F32)


def eye(n):
    same = lax.broadcasted_iota(jnp.int32, (n, n), 0) == lax.broadcasted_iota(jnp.int32, (n, n), 1)
    return same.astype(F32).astype(BF16)


def call(body, out, operands, flops=0, core=None):
    scalar = () if core is None else (core,)
    specs = [pl.BlockSpec(memory_space=pltpu.SMEM)] * len(scalar) + [VMEM] * len(operands)
    moved = sum(math.prod(o.shape) * o.dtype.itemsize for o in (*operands, *jax.tree.leaves(out)))
    return pl.pallas_call(
        body,
        out_shape=out,
        in_specs=specs,
        out_specs=jax.tree.map(lambda _: VMEM, out),
        compiler_params=pltpu.CompilerParams(vmem_limit_bytes=40 * 2**20),
        cost_estimate=pl.CostEstimate(flops=flops, bytes_accessed=moved, transcendentals=0),
    )(*scalar, *operands)


def place_kernel(capacity, tokens_ref, routes_ref, weight_ref, placed_ref, mix_ref):
    top, rows = routes_ref.shape
    slots = placed_ref.shape[0]
    slot = lax.broadcasted_iota(jnp.int32, (slots, rows), 0)
    expert = slot // capacity
    spot = slot % capacity
    weight = weight_ref[...].astype(F32)
    share = weight / jnp.sum(weight, axis=0, keepdims=True)
    named = jnp.zeros((slots, rows), F32)
    mix = jnp.zeros((slots, rows), F32)
    for k in range(top):
        hit = routes_ref[k : k + 1, :] == expert
        named += jnp.where(hit, 1.0, 0.0)
        mix += jnp.where(hit, share[k : k + 1, :], 0.0)
    earlier = lax.broadcasted_iota(jnp.int32, (rows, rows), 0) < lax.broadcasted_iota(jnp.int32, (rows, rows), 1)
    before = dot(named.astype(BF16), earlier.astype(F32).astype(BF16), ((1,), (0,)))
    here = (named > 0.5) & (before.astype(jnp.int32) == spot)
    mix_ref[...] = jnp.where(here, mix, 0.0)
    dispatch = jnp.where(here, 1.0, 0.0).astype(BF16)
    placed_ref[...] = dot(dispatch, tokens_ref[...], ((1,), (0,))).astype(BF16)


def turn_kernel(arrived_ref, copies_ref):
    n, depth, _ = copies_ref.shape
    turned = dot(eye(depth), arrived_ref[...], ((1,), (1,))).astype(BF16)
    for i in range(n):
        copies_ref[i] = turned


def split_kernel(depth, core_ref, gate_ref, up_ref, down_ref, own_ref, send_ref):
    group = 4
    wide = 2 * group * depth
    thin = group * depth
    source = lax.broadcasted_iota(jnp.int32, (wide, thin), 0)
    target = lax.broadcasted_iota(jnp.int32, (wide, thin), 1)
    first = target + (target // depth) * depth
    own_pick = (source == first + core_ref[0] * depth).astype(F32).astype(BF16)
    send_pick = (source == first + (1 - core_ref[0]) * depth).astype(F32).astype(BF16)
    for k, ref in enumerate((gate_ref, up_ref, down_ref)):
        for g in range(ref.shape[1] // wide):
            block = ref[:, g * wide : (g + 1) * wide]
            own_ref[k, :, g * thin : (g + 1) * thin] = dot(block, own_pick, ((1,), (0,))).astype(BF16)
            send_ref[k, :, g * thin : (g + 1) * thin] = dot(block, send_pick, ((1,), (0,))).astype(BF16)


def stack_kernel(core_ref, own_ref, got_ref, rise_ref, fall_ref):
    units = own_ref.shape[1]
    pad = rise_ref.shape[1] - units
    for ref, which in ((own_ref, core_ref[0]), (got_ref, 1 - core_ref[0])):
        for k in range(2):
            rise_ref[2 * which + k, :units] = ref[k]
            rise_ref[2 * which + k, units:] = jnp.zeros((pad, rise_ref.shape[2]), BF16)
        fall_ref[which] = ref[2].T


def rise_kernel(x_ref, rise_ref, out_ref):
    n, units, slots = out_ref.shape
    padded = rise_ref.shape[0] // n
    product = dot(rise_ref[...], x_ref[...], ((1,), (0,)))
    for k in range(n):
        out_ref[k] = product[k * padded : k * padded + units].astype(BF16)


def fall_kernel(halves_ref, fall_ref, out_ref):
    hidden = []
    for u in range(2):
        gate = halves_ref[2 * u].astype(F32) + halves_ref[4 + 2 * u].astype(F32)
        up = halves_ref[2 * u + 1].astype(F32) + halves_ref[5 + 2 * u].astype(F32)
        hidden.append((gate / (1.0 + jnp.exp(-gate)) * up).astype(BF16))
    chunk = 384
    for i in range(out_ref.shape[0] // chunk):
        at = slice(i * chunk, (i + 1) * chunk)
        part = dot(fall_ref[0, at], hidden[0], ((1,), (0,))) + dot(fall_ref[1, at], hidden[1], ((1,), (0,)))
        out_ref[at] = part.astype(BF16)


def sum_kernel(pieces_ref, out_ref):
    n, depth, _ = pieces_ref.shape
    total = pieces_ref[0].astype(F32)
    for i in range(1, n):
        total += pieces_ref[i].astype(F32)
    out_ref[...] = dot(total.astype(BF16), eye(depth), ((0,), (0,))).astype(BF16)


def mix_kernel(mix_ref, returned_ref, out_ref):
    rest = mix_ref[...]
    values = returned_ref[...]
    total = jnp.zeros(out_ref.shape, F32)
    for _ in range(3):
        piece = rest.astype(BF16)
        rest = rest - piece.astype(F32)
        total += dot(piece, values, ((0,), (0,)))
    out_ref[...] = total.astype(BF16)


def local(tokens, routes, route_weight, w_gate, w_up, w_down):
    experts, chips = lax.axis_size("expert"), lax.axis_size(GRID)
    rows, depth = tokens.shape
    units, width = w_gate.shape[1:]
    half = width // 2
    padded = -(-units // 16) * 16
    capacity = min(rows, 2 * rows * routes.shape[1] // experts)
    slots = experts * capacity
    core = lax.axis_index("core").astype(jnp.int32).reshape(1)

    def shape(*dims, dtype=BF16):
        return jax.ShapeDtypeStruct(dims, dtype)

    placed, mix = call(
        functools.partial(place_kernel, capacity),
        (shape(slots, depth), shape(slots, rows, dtype=F32)),
        (tokens, routes.T, route_weight.T),
    )
    arrived = lax.all_to_all(placed.reshape(experts, capacity, depth), "expert", 0, 0, tiled=True)

    thirds = shape(3, units, half)
    own, send = call(
        functools.partial(split_kernel, depth),
        (thirds, thirds),
        (w_gate[0], w_up[0], w_down[0]),
        flops=3 * 2 * 2 * units * half * 8 * depth,
        core=core,
    )
    got = lax.ppermute(send, "core", ((0, 1), (1, 0)))
    rise, fall = call(stack_kernel, (shape(4, padded, half), shape(2, half, units)), (own, got), core=core)

    copies = call(turn_kernel, shape(chips, depth, slots), (arrived.reshape(slots, depth),))
    x = lax.all_to_all(copies, GRID, 0, 0, tiled=True).reshape(half, slots)
    partial = call(
        rise_kernel,
        shape(4, units, slots),
        (x, rise.reshape(4 * padded, half)),
        flops=2 * 4 * padded * half * slots,
    )
    halves = lax.all_gather(partial, "core", axis=0, tiled=True)
    part = call(fall_kernel, shape(half, slots), (halves, fall), flops=2 * 2 * units * half * slots)
    pieces = lax.all_to_all(part.reshape(chips, depth, slots), GRID, 0, 0, tiled=True)
    summed = call(sum_kernel, shape(slots, depth), (pieces,))
    returned = lax.all_to_all(summed.reshape(experts, capacity, depth), "expert", 0, 0, tiled=True)
    return call(mix_kernel, shape(rows, depth), (mix, returned.reshape(slots, depth)))


def solution(mesh):
    chips_y = chips_x = 4
    devices = mesh.devices
    fine = Mesh(devices.reshape(devices.shape[0], chips_y, chips_x, 2), ("expert", "y", "x", "core"))
    tensor = ("y", "x", "core")
    placed = (
        P("expert", tensor),
        P("expert", None),
        P("expert", None),
        P("expert", tensor, None),
        P("expert", tensor, None),
        P("expert", tensor, None),
    )
    return jax.shard_map(local, mesh=fine, in_specs=placed, out_specs=P("expert", tensor), check_vma=False)
```

time: 96.6 us -> 100 us (1.035)
  blocking collectives: 80.4 us -> 65.2 us
  local copies, waits for them, and re-layouts: 2.7 us -> 9.94 us
  starting transfers between devices: 3.95 us -> 9.38 us
  Pallas kernels: 4.52 us -> 9.26 us
  waiting for transfers between devices: 4.51 us -> 5.93 us
    all_to_all x2 -> x1, blocking collectives: 36.5 us -> 17.7 us  [local(): lax.all_to_all(part.reshape(chips, depth, slots), GRID, 0, 0, tiled=True)]
    all_to_all x0 -> x1, starting transfers between devices: none -> 7.48 us  [local(): x = lax.all_to_all(copies, GRID, 0, 0, tiled=True).reshape(half, slots)]
    unnamed x12 -> x24, local copies, waits for them, and re-layouts: 2.7 us -> 9.94 us
    all_to_all x0 -> x1, waiting for transfers between devices: none -> 5.93 us  [local(): x = lax.all_to_all(copies, GRID, 0, 0, tiled=True).reshape(half, slots)]
    pallas_call x6 -> x8, Pallas kernels: 4.52 us -> 9.26 us  [call(): pl.pallas_call(body, out_shape=out, in_specs=specs, out_specs=jax.tree.ma...]
    ppermute x2 -> x1, waiting for transfers between devices: 4.51 us -> 0.01 us  [local(): got = lax.ppermute(send, 'core', ((0, 1), (1, 0)))]
    all_gather x0 -> x1, blocking collectives: none -> 2.3 us  [local(): halves = lax.all_gather(partial, 'core', axis=0, tiled=True)]
    ppermute x2 -> x1, starting transfers between devices: 3.95 us -> 1.91 us  [local(): got = lax.ppermute(send, 'core', ((0, 1), (1, 0)))]
  transfers between devices with their start and end apart: 2 -> 2, of which waited for: 2 -> 1; matrix products, arithmetic and copies ran while one was open for 0% -> 0% of each run, Pallas kernels for 0% -> 2%
where the time goes in v2:
time: 100 us; the launch traced here: 99.8 us
  blocking collectives  65.2 us (65%)
  local copies, waits for them, and re-layouts  9.94 us (10%)
  starting transfers between devices  9.38 us (9%)
  Pallas kernels  9.26 us (9%)
  waiting for transfers between devices  5.93 us (6%)
    all_to_all x1, blocking collectives, local(): lax.all_to_all(placed.reshape(experts, capacity, depth), 'expert', 0, 0,...  28.4 us
    all_to_all x1, blocking collectives, local(): lax.all_to_all(part.reshape(chips, depth, slots), GRID, 0, 0, tiled=True)  17.7 us
    all_to_all x1, blocking collectives, local(): lax.all_to_all(summed.reshape(experts, capacity, depth), 'expert', 0, 0,...  16.8 us
    unnamed x24, local copies, waits for them, and re-layouts  9.94 us
    pallas_call x8, Pallas kernels, call(): pl.pallas_call(body, out_shape=out, in_specs=specs, out_specs=jax.tree.ma...  9.26 us
    all_to_all x1, starting transfers between devices, local(): x = lax.all_to_all(copies, GRID, 0, 0, tiled=True).reshape(half, slots)  7.48 us
    all_to_all x1, waiting for transfers between devices, local(): x = lax.all_to_all(copies, GRID, 0, 0, tiled=True).reshape(half, slots)  5.93 us
    all_gather x1, blocking collectives, local(): halves = lax.all_gather(partial, 'core', axis=0, tiled=True)  2.3 us
  transfers between devices with their start and end apart: 2, of which 1 were waited for; matrix products, arithmetic and copies ran while one was open for 0% of the time, Pallas kernels for 2%

profile of v2, /device:TPU:2, one launch (start us, length us, event | category | flops | bytes accessed | tf_op | source)
XLA Modules:
  0.0 99.8 jit_solution(11659306393637619776)
XLA Ops:
  0.0 0.0 copy-start.9
  0.0 1.2 %copy-done.9 = bf16[1,168,3072]{2,1,0:T(8,128)(2,1)S(1)} copy-done((bf16[1,168,3072]{2,1,0:T(8,128)(2,1)S(1)}, bf16[1,168,3072]{2,1,0:T(8,128)(2,1)}, u32[]{:S(2)}) %copy-start.9) | copy-done | bytes 1032216
  1.2 0.0 copy-start.10
  1.2 1.2 %copy-done.10 = bf16[1,168,3072]{2,1,0:T(8,128)(2,1)S(1)} copy-done((bf16[1,168,3072]{2,1,0:T(8,128)(2,1)S(1)}, bf16[1,168,3072]{2,1,0:T(8,128)(2,1)}, u32[]{:S(2)}) %copy-start.10) | copy-done | bytes 1032216
  2.4 0.0 copy-start.11
  2.4 1.2 %copy-done.11 = bf16[1,168,3072]{2,1,0:T(8,128)(2,1)S(1)} copy-done((bf16[1,168,3072]{2,1,0:T(8,128)(2,1)S(1)}, bf16[1,168,3072]{2,1,0:T(8,128)(2,1)}, u32[]{:S(2)}) %copy-start.11) | copy-done | bytes 1032216
  3.7 0.0 copy-start.6
  3.7 0.0 copy-start.7
  3.7 0.0 copy-start.8
  3.7 4.7 %shard_map.66 = (bf16[3,168,1536]{2,1,0:T(8,128)(2,1)S(1)}, bf16[3,168,1536]{2,1,0:T(8,128)(2,1)}) custom-call(s32[1]{0:T(128)} %bitcast.5.core_ref, bf16[168,3072]{1,0:T(8,128)(2,1)S(1)} %bitcast.22, bf16[168,3072]{1,0:T(8,128)(2,1)S(1)} %bitcast.23, bf16[168,3072]{1,0:T(8,128)(2,1)S(1)} %bitcast.24), custom_call_target="tpu_custom_call" | custom-call | flops 2378170368 | bytes 6193152 | tf_op jit(solution)/shard_map/pallas_call | solution.py:30
  8.4 0.0 copy-start.2
  8.4 1.2 %copy-done.2 = bf16[3,168,1536]{2,1,0:T(8,128)(2,1)} copy-done((bf16[3,168,1536]{2,1,0:T(8,128)(2,1)}, bf16[3,168,1536]{2,1,0:T(8,128)(2,1)S(1)}, u32[]{:S(2)}) %copy-start.2) | copy-done | bytes 1548312
  9.6 1.9 %collective-permute-start = (bf16[3,168,1536]{2,1,0:T(8,128)(2,1)}, bf16[3,168,1536]{2,1,0:T(8,128)(2,1)S(1)}, u32[]{:S(2)}, u32[]{:S(2)}) collective-permute-start(bf16[3,168,1536]{2,1,0:T(8,128)(2,1)} %get-tuple-element.14), channel_id=1, source_target_pairs={{0,1},{1,0},{2,3},{3,2},{4,5},{5,4},{6,7},{7,6},{8,9},{9,8},{10,11... | collective-permute-start | bytes 4644872 | tf_op jit(solution)/shard_map/ppermute | solution.py:163
  11.5 0.0 copy-done.6
  11.5 0.0 copy-done.7
  11.5 0.0 copy-done.8
  11.5 0.3 shard_map.64
  11.8 28.4 %all_to_all.20 = bf16[16,16,96]{2,1,0:T(8,128)(2,1)S(1)} all-to-all(bf16[16,16,96]{2,1,0:T(8,128)(2,1)S(1)} %bitcast.19), channel_id=1, replica_groups=mesh['expert'=16,'y'=4,'x'=4,'core'=2] {'expert'}, dimensions={0} | all-to-all | bytes 98304 | tf_op jit(solution)/shard_map/all_to_all | solution.py:153
  40.2 1.1 %shard_map.65 = bf16[16,96,256]{2,1,0:T(8,128)(2,1)} custom-call(bf16[256,96]{1,0:T(8,128)(2,1)S(1)} %bitcast.17), custom_call_target="tpu_custom_call" | custom-call | bytes 835584 | tf_op jit(solution)/shard_map/pallas_call | solution.py:30
  41.3 7.5 %all-to-all-start.1 = ((bf16[16,96,256]{2,1,0:T(8,128)(2,1)}), bf16[16,96,256]{2,1,0:T(8,128)(2,1)S(1)}, u32[]{:S(2)}, u32[]{:S(2)}) async-start(bf16[16,96,256]{2,1,0:T(8,128)(2,1)} %shard_map.65), calls=%async_computation.1 | async-start | bytes 1572864 | tf_op jit(solution)/shard_map/all_to_all | solution.py:167
  48.8 0.0 collective-permute-done.got_ref
  48.8 0.0 copy-start.4
  48.8 1.1 %copy-done.4 = bf16[3,168,1536]{2,1,0:T(8,128)(2,1)} copy-done((bf16[3,168,1536]{2,1,0:T(8,128)(2,1)}, bf16[3,168,1536]{2,1,0:T(8,128)(2,1)S(1)}, u32[]{:S(2)}) %copy-start.4) | copy-done | bytes 1548312
  49.9 0.0 copy-start.3
  49.9 1.4 %copy-done.3 = bf16[3,168,1536]{2,1,0:T(8,128)(2,1)S(1)} copy-done((bf16[3,168,1536]{2,1,0:T(8,128)(2,1)S(1)}, bf16[3,168,1536]{2,1,0:T(8,128)(2,1)}, u32[]{:S(2)}) %copy-start.3) | copy-done | bytes 1548312
  51.3 0.0 copy-start.5
  51.3 1.4 %copy-done.5 = bf16[3,168,1536]{2,1,0:T(8,128)(2,1)S(1)} copy-done((bf16[3,168,1536]{2,1,0:T(8,128)(2,1)S(1)}, bf16[3,168,1536]{2,1,0:T(8,128)(2,1)}, u32[]{:S(2)}) %copy-start.5) | copy-done | bytes 1548312
  52.7 0.6 shard_map.67
  53.4 0.0 copy-start
  53.4 1.2 %copy-done = bf16[2,1536,168]{2,1,0:T(8,128)(2,1)} copy-done((bf16[2,1536,168]{2,1,0:T(8,128)(2,1)}, bf16[2,1536,168]{2,1,0:T(8,128)(2,1)S(1)}, u32[]{:S(2)}) %copy-start) | copy-done | bytes 1032216
  54.6 5.9 %all-to-all-done.1 = bf16[16,96,256]{2,1,0:T(8,128)(2,1)S(1)} async-done(((bf16[16,96,256]{2,1,0:T(8,128)(2,1)}), bf16[16,96,256]{2,1,0:T(8,128)(2,1)S(1)}, u32[]{:S(2)}, u32[]{:S(2)}) %all-to-all-start.1) | async-done | bytes 786464 | tf_op jit(solution)/shard_map/all_to_all | solution.py:167
  60.5 0.0 copy-start.1
  60.5 0.7 shard_map.68
  61.2 2.3 %all_gather.3.halves_ref = bf16[8,168,256]{2,1,0:T(8,128)(2,1)S(1)} all-gather(bf16[4,168,256]{2,1,0:T(8,128)(2,1)S(1)} %shard_map.68), channel_id=1, replica_groups=mesh['expert'=16,'y'=4,'x'=4,'core'=2] {'core'}, dimensions={0}, use_global_device_ids=true | all-gather | bytes 1032192 | tf_op jit(solution)/shard_map/all_gather | solution.py:174
  63.5 0.0 copy-done.1
  63.5 0.6 shard_map.69
  64.2 17.7 %all_to_all.21.pieces_ref = bf16[16,96,256]{2,1,0:T(8,128)(2,1)S(1)} all-to-all(bf16[16,96,256]{2,1,0:T(8,128)(2,1)S(1)} %bitcast.14), channel_id=1, replica_groups=mesh['expert'=16,'y'=4,'x'=4,'core'=2] {'y','x'}, dimensions={0} | all-to-all | bytes 1572864 | tf_op jit(solution)/shard_map/all_to_all | solution.py:176
  81.8 0.3 shard_map.70
  82.1 16.8 %all_to_all.22 = bf16[16,16,96]{2,1,0:T(8,128)(2,1)S(1)} all-to-all(bf16[16,16,96]{2,1,0:T(8,128)(2,1)S(1)} %bitcast.18), channel_id=1, replica_groups=mesh['expert'=16,'y'=4,'x'=4,'core'=2] {'expert'}, dimensions={0} | all-to-all | bytes 98304 | tf_op jit(solution)/shard_map/all_to_all | solution.py:178
  98.9 0.8 shard_map.71
Async XLA Ops:
  0.0 1.2 %copy-start.9 = (bf16[1,168,3072]{2,1,0:T(8,128)(2,1)S(1)}, bf16[1,168,3072]{2,1,0:T(8,128)(2,1)}, u32[]{:S(2)}) copy-start(bf16[1,168,3072]{2,1,0:T(8,128)(2,1)} %param.9) | copy-start | bytes 3096580
  1.2 1.2 %copy-start.10 = (bf16[1,168,3072]{2,1,0:T(8,128)(2,1)S(1)}, bf16[1,168,3072]{2,1,0:T(8,128)(2,1)}, u32[]{:S(2)}) copy-start(bf16[1,168,3072]{2,1,0:T(8,128)(2,1)} %param.10) | copy-start | bytes 3096580
  2.4 1.2 %copy-start.11 = (bf16[1,168,3072]{2,1,0:T(8,128)(2,1)S(1)}, bf16[1,168,3072]{2,1,0:T(8,128)(2,1)}, u32[]{:S(2)}) copy-start(bf16[1,168,3072]{2,1,0:T(8,128)(2,1)} %param.11) | copy-start | bytes 3096580
  3.7 7.8 %copy-start.6 = (bf16[32,96]{1,0:T(8,128)(2,1)S(1)}, bf16[32,96]{1,0:T(8,128)(2,1)}, u32[]{:S(2)}) copy-start(bf16[32,96]{1,0:T(8,128)(2,1)} %tokens_ref.1) | copy-start | bytes 18436
  3.7 7.8 %copy-start.7 = (s32[32,4]{0,1:T(4,128)S(1)}, s32[32,4]{0,1:T(4,128)}, u32[]{:S(2)}) copy-start(s32[32,4]{0,1:T(4,128)} %param.7) | copy-start | bytes 1540
  3.7 7.8 %copy-start.8 = (s32[32,4]{0,1:T(4,128)S(1)}, s32[32,4]{0,1:T(4,128)}, u32[]{:S(2)}) copy-start(s32[32,4]{0,1:T(4,128)} %param.8) | copy-start | bytes 1540
  8.4 1.2 %copy-start.2 = (bf16[3,168,1536]{2,1,0:T(8,128)(2,1)}, bf16[3,168,1536]{2,1,0:T(8,128)(2,1)S(1)}, u32[]{:S(2)}) copy-start(bf16[3,168,1536]{2,1,0:T(8,128)(2,1)S(1)} %get-tuple-element.13.own_ref) | copy-start | bytes 4644868
  9.6 39.2 %collective-permute-start = (bf16[3,168,1536]{2,1,0:T(8,128)(2,1)}, bf16[3,168,1536]{2,1,0:T(8,128)(2,1)S(1)}, u32[]{:S(2)}, u32[]{:S(2)}) collective-permute-start(bf16[3,168,1536]{2,1,0:T(8,128)(2,1)} %get-tuple-element.14), channel_id=1, source_target_pairs={{0,1},{1,0},{2,3},{3,2},{4,5},{5,4},{6,7},{7,6},{8,9},{9,8},{10,11... | collective-permute-start | bytes 4644872 | tf_op jit(solution)/shard_map/ppermute | solution.py:163
  41.3 19.2 %all-to-all-start.1 = ((bf16[16,96,256]{2,1,0:T(8,128)(2,1)}), bf16[16,96,256]{2,1,0:T(8,128)(2,1)S(1)}, u32[]{:S(2)}, u32[]{:S(2)}) async-start(bf16[16,96,256]{2,1,0:T(8,128)(2,1)} %shard_map.65), calls=%async_computation.1 | async-start | bytes 1572864 | tf_op jit(solution)/shard_map/all_to_all | solution.py:167
  48.8 1.1 %copy-start.4 = (bf16[3,168,1536]{2,1,0:T(8,128)(2,1)}, bf16[3,168,1536]{2,1,0:T(8,128)(2,1)S(1)}, u32[]{:S(2)}) copy-start(bf16[3,168,1536]{2,1,0:T(8,128)(2,1)S(1)} %collective-permute-done.got_ref) | copy-start | bytes 4644868
  49.9 1.4 %copy-start.3 = (bf16[3,168,1536]{2,1,0:T(8,128)(2,1)S(1)}, bf16[3,168,1536]{2,1,0:T(8,128)(2,1)}, u32[]{:S(2)}) copy-start(bf16[3,168,1536]{2,1,0:T(8,128)(2,1)} %copy-done.2) | copy-start | bytes 4644868
  51.3 1.4 %copy-start.5 = (bf16[3,168,1536]{2,1,0:T(8,128)(2,1)S(1)}, bf16[3,168,1536]{2,1,0:T(8,128)(2,1)}, u32[]{:S(2)}) copy-start(bf16[3,168,1536]{2,1,0:T(8,128)(2,1)} %copy-done.4) | copy-start | bytes 4644868
  53.4 1.2 %copy-start = (bf16[2,1536,168]{2,1,0:T(8,128)(2,1)}, bf16[2,1536,168]{2,1,0:T(8,128)(2,1)S(1)}, u32[]{:S(2)}) copy-start(bf16[2,1536,168]{2,1,0:T(8,128)(2,1)S(1)} %get-tuple-element.16.fall_ref) | copy-start | bytes 3096580
  60.5 3.0 %copy-start.1 = (bf16[2,1536,168]{2,1,0:T(8,128)(2,1)S(1)}, bf16[2,1536,168]{2,1,0:T(8,128)(2,1)}, u32[]{:S(2)}) copy-start(bf16[2,1536,168]{2,1,0:T(8,128)(2,1)} %copy-done) | copy-start | bytes 3096580

commit v3 on v2

--- a/solution.py
+++ b/solution.py
@@ -10,6 +10,7 @@
 
 GRID = ("y", "x")
 VMEM = pl.BlockSpec(memory_space=pltpu.VMEM)
+ANY = pl.BlockSpec(memory_space=pltpu.HBM)
 BF16 = jnp.bfloat16
 F32 = jnp.float32
 
@@ -23,21 +24,35 @@
     return same.astype(F32).astype(BF16)
 
 
-def call(body, out, operands, flops=0, core=None):
+def call(body, out, operands, flops=0, core=None, far=(), aliases={}, far_out=0, scratch=(), cost=True, grant=20480):
     scalar = () if core is None else (core,)
-    specs = [pl.BlockSpec(memory_space=pltpu.SMEM)] * len(scalar) + [VMEM] * len(operands)
-    moved = sum(math.prod(o.shape) * o.dtype.itemsize for o in (*operands, *jax.tree.leaves(out)))
+    specs = [pl.BlockSpec(memory_space=pltpu.SMEM)] * len(scalar) + [VMEM] * len(operands) + [ANY] * len(far)
+    outs = jax.tree.leaves(out)
+    moved = sum(math.prod(o.shape) * o.dtype.itemsize for o in (*operands, *outs))
+    out_specs = [VMEM] * (len(outs) - far_out) + [ANY] * far_out
     return pl.pallas_call(
         body,
         out_shape=out,
         in_specs=specs,
-        out_specs=jax.tree.map(lambda _: VMEM, out),
-        compiler_params=pltpu.CompilerParams(vmem_limit_bytes=40 * 2**20),
-        cost_estimate=pl.CostEstimate(flops=flops, bytes_accessed=moved, transcendentals=0),
-    )(*scalar, *operands)
-
-
-def place_kernel(capacity, tokens_ref, routes_ref, weight_ref, placed_ref, mix_ref):
+        out_specs=tuple(out_specs) if isinstance(out, tuple) else out_specs[0],
+        input_output_aliases=aliases,
+        scratch_shapes=list(scratch),
+        compiler_params=pltpu.CompilerParams(vmem_limit_bytes=grant * 2**10),
+        cost_estimate=pl.CostEstimate(flops=flops * cost, bytes_accessed=moved * cost, transcendentals=0),
+    )(*scalar, *operands, *far)
+
+
+def fetch(pairs, sems):
+    copies = [pltpu.make_async_copy(source, target, sems.at[i]) for i, (source, target) in enumerate(pairs)]
+    for copy in copies:
+        copy.start()
+    return copies
+
+
+def place_kernel(capacity, tokens_far, routes_far, weight_far, placed_ref, mix_ref, tokens_ref, routes_ref, weight_ref, sems):
+    pairs = ((tokens_far, tokens_ref), (routes_far, routes_ref), (weight_far, weight_ref))
+    for copy in fetch(pairs, sems):
+        copy.wait()
     top, rows = routes_ref.shape
     slots = placed_ref.shape[0]
     slot = lax.broadcasted_iota(jnp.int32, (slots, rows), 0)
@@ -59,37 +74,70 @@
     placed_ref[...] = dot(dispatch, tokens_ref[...], ((1,), (0,))).astype(BF16)
 
 
-def turn_kernel(arrived_ref, copies_ref):
+def turn_kernel(arrived_ref, _, copies_ref, __):
     n, depth, _ = copies_ref.shape
     turned = dot(eye(depth), arrived_ref[...], ((1,), (1,))).astype(BF16)
     for i in range(n):
         copies_ref[i] = turned
 
 
-def split_kernel(depth, core_ref, gate_ref, up_ref, down_ref, own_ref, send_ref):
-    group = 4
-    wide = 2 * group * depth
-    thin = group * depth
+def picker(depth, group, which):
+    wide, thin = 2 * group * depth, group * depth
     source = lax.broadcasted_iota(jnp.int32, (wide, thin), 0)
     target = lax.broadcasted_iota(jnp.int32, (wide, thin), 1)
-    first = target + (target // depth) * depth
-    own_pick = (source == first + core_ref[0] * depth).astype(F32).astype(BF16)
-    send_pick = (source == first + (1 - core_ref[0]) * depth).astype(F32).astype(BF16)
-    for k, ref in enumerate((gate_ref, up_ref, down_ref)):
-        for g in range(ref.shape[1] // wide):
-            block = ref[:, g * wide : (g + 1) * wide]
-            own_ref[k, :, g * thin : (g + 1) * thin] = dot(block, own_pick, ((1,), (0,))).astype(BF16)
-            send_ref[k, :, g * thin : (g + 1) * thin] = dot(block, send_pick, ((1,), (0,))).astype(BF16)
-
-
-def stack_kernel(core_ref, own_ref, got_ref, rise_ref, fall_ref):
-    units = own_ref.shape[1]
+    return (source == target + (target // depth + which) * depth).astype(F32).astype(BF16)
+
+
+def pick_kernel(depth, core_ref, gate_far, up_far, down_far, _, send_far, weights_ref, send_ref, sems, out_sems):
+    loads = fetch([(far, weights_ref.at[k]) for k, far in enumerate((gate_far, up_far, down_far))], sems)
+    wide, thin = 8 * depth, 4 * depth
+    pick = picker(depth, 4, 1 - core_ref[0])
+    stores = []
+    for k, load in enumerate(loads):
+        load.wait()
+        for g in range(weights_ref.shape[2] // wide):
+            block = weights_ref[k, :, g * wide : (g + 1) * wide]
+            send_ref[k, :, g * thin : (g + 1) * thin] = dot(block, pick, ((1,), (0,))).astype(BF16)
+        store = pltpu.make_async_copy(send_ref.at[k], send_far.at[k], out_sems.at[k])
+        store.start()
+        stores.append(store)
+    for store in stores:
+        store.wait()
+
+
+def stack_kernel(
+    depth, core_ref, gate_far, up_far, down_far, got_far, rise_ref, fall_far, weights_ref, got_ref, fall_ref, sems
+):
+    pairs = [(far, weights_ref.at[k]) for k, far in enumerate((gate_far, up_far, down_far))]
+    loads = fetch(pairs + [(got_far.at[k], got_ref.at[k]) for k in range(3)], sems)
+    units = got_ref.shape[1]
     pad = rise_ref.shape[1] - units
-    for ref, which in ((own_ref, core_ref[0]), (got_ref, 1 - core_ref[0])):
-        for k in range(2):
-            rise_ref[2 * which + k, :units] = ref[k]
-            rise_ref[2 * which + k, units:] = jnp.zeros((pad, rise_ref.shape[2]), BF16)
-        fall_ref[which] = ref[2].T
+    wide, thin = 8 * depth, 4 * depth
+    own, other = core_ref[0], 1 - core_ref[0]
+    pick = picker(depth, 4, own)
+    for k in range(4):
+        rise_ref[k, units:] = jnp.zeros((pad, rise_ref.shape[2]), BF16)
+    stores = [pltpu.make_async_copy(fall_ref.at[u], fall_far.at[u], sems.at[6 + i]) for i, u in enumerate((own, other))]
+    for k in reversed(range(3)):
+        loads[k].wait()
+        for g in range(weights_ref.shape[2] // wide):
+            block = weights_ref[k, :, g * wide : (g + 1) * wide]
+            chosen = dot(block, pick, ((1,), (0,))).astype(BF16)
+            if k < 2:
+                rise_ref[2 * own + k, :units, g * thin : (g + 1) * thin] = chosen
+            else:
+                fall_ref[own, g * thin : (g + 1) * thin] = chosen.T
+        if k == 2:
+            stores[0].start()
+    for k in reversed(range(3)):
+        loads[3 + k].wait()
+        if k < 2:
+            rise_ref[2 * other + k, :units] = got_ref[k]
+        else:
+            fall_ref[other] = got_ref[k].T
+            stores[1].start()
+    for store in stores:
+        store.wait()
 
 
 def rise_kernel(x_ref, rise_ref, out_ref):
@@ -148,22 +196,54 @@
     placed, mix = call(
         functools.partial(place_kernel, capacity),
         (shape(slots, depth), shape(slots, rows, dtype=F32)),
-        (tokens, routes.T, route_weight.T),
+        (),
+        far=(tokens, routes.T, route_weight.T),
+        scratch=(
+            pltpu.VMEM(tokens.shape, tokens.dtype),
+            pltpu.VMEM(routes.shape[::-1], routes.dtype),
+            pltpu.VMEM(routes.shape[::-1], route_weight.dtype),
+            pltpu.SemaphoreType.DMA((3,)),
+        ),
+        grant=65536,
     )
     arrived = lax.all_to_all(placed.reshape(experts, capacity, depth), "expert", 0, 0, tiled=True)
 
+    weights = (w_gate[0], w_up[0], w_down[0])
     thirds = shape(3, units, half)
-    own, send = call(
-        functools.partial(split_kernel, depth),
-        (thirds, thirds),
-        (w_gate[0], w_up[0], w_down[0]),
-        flops=3 * 2 * 2 * units * half * 8 * depth,
+    whole_ref, third_ref = pltpu.VMEM((3, units, width), BF16), pltpu.VMEM(thirds.shape, BF16)
+    picking = 3 * 2 * units * half * 8 * depth
+    send = call(
+        functools.partial(pick_kernel, depth),
+        thirds,
+        (),
+        flops=picking,
         core=core,
+        far=(*weights, placed),
+        far_out=1,
+        scratch=(whole_ref, third_ref, pltpu.SemaphoreType.DMA((3,)), pltpu.SemaphoreType.DMA((3,))),
+        grant=65024,
+    )
+    copies, send = call(
+        turn_kernel,
+        (shape(chips, depth, slots), thirds),
+        (arrived.reshape(slots, depth),),
+        far=(send,),
+        aliases={1: 1},
+        far_out=1,
     )
     got = lax.ppermute(send, "core", ((0, 1), (1, 0)))
-    rise, fall = call(stack_kernel, (shape(4, padded, half), shape(2, half, units)), (own, got), core=core)
-
-    copies = call(turn_kernel, shape(chips, depth, slots), (arrived.reshape(slots, depth),))
+    rise, fall = call(
+        functools.partial(stack_kernel, depth),
+        (shape(4, padded, half), shape(2, half, units)),
+        (),
+        core=core,
+        far=(*weights, got),
+        far_out=1,
+        scratch=(whole_ref, third_ref, pltpu.VMEM((2, half, units), BF16), pltpu.SemaphoreType.DMA((8,))),
+        cost=False,
+        grant=61440,
+    )
+
     x = lax.all_to_all(copies, GRID, 0, 0, tiled=True).reshape(half, slots)
     partial = call(
         rise_kernel,

time: 100 us -> 94.8 us (0.948)
  blocking collectives: 65.2 us -> 36.3 us
  starting transfers between devices: 9.38 us -> 24.6 us
  waiting for transfers between devices: 5.93 us -> 14.3 us
  local copies, waits for them, and re-layouts: 9.94 us -> 2.76 us
  Pallas kernels: 9.26 us -> 16.2 us
    all_to_all x1 -> x0, blocking collectives: 28.4 us -> none  [local(): lax.all_to_all(placed.reshape(experts, capacity, depth), 'expert', 0, 0,...]
    all_to_all x0 -> x1, starting transfers between devices: none -> 15.2 us  [local(): lax.all_to_all(placed.reshape(experts, capacity, depth), 'expert', 0, 0,...]
    all_to_all x0 -> x1, waiting for transfers between devices: none -> 8.47 us  [local(): lax.all_to_all(placed.reshape(experts, capacity, depth), 'expert', 0, 0,...]
    unnamed x24 -> x8, local copies, waits for them, and re-layouts: 9.94 us -> 2.76 us
    pallas_call x8, Pallas kernels: 9.26 us -> 16.2 us  [call(): pl.pallas_call(body, out_shape=out, in_specs=specs, out_specs=tuple(out_s...]
  transfers between devices with their start and end apart: 2 -> 3, of which waited for: 1 -> 2; matrix products, arithmetic and copies ran while one was open for 0% -> 0% of each run, Pallas kernels for 2% -> 12%
where the time goes in v3:
time: 94.8 us; the launch traced here: 94.3 us
  blocking collectives  36.3 us (38%)
  starting transfers between devices  24.6 us (26%)
  Pallas kernels  16.2 us (17%)
  waiting for transfers between devices  14.3 us (15%)
  local copies, waits for them, and re-layouts  2.76 us (3%)
    all_to_all x1, blocking collectives, local(): lax.all_to_all(part.reshape(chips, depth, slots), GRID, 0, 0, tiled=True)  17.8 us
    all_to_all x1, blocking collectives, local(): lax.all_to_all(summed.reshape(experts, capacity, depth), 'expert', 0, 0,...  16.2 us
    pallas_call x8, Pallas kernels, call(): pl.pallas_call(body, out_shape=out, in_specs=specs, out_specs=tuple(out_s...  16.2 us
    all_to_all x1, starting transfers between devices, local(): lax.all_to_all(placed.reshape(experts, capacity, depth), 'expert', 0, 0,...  15.2 us
    all_to_all x1, waiting for transfers between devices, local(): lax.all_to_all(placed.reshape(experts, capacity, depth), 'expert', 0, 0,...  8.47 us
    all_to_all x1, starting transfers between devices, local(): x = lax.all_to_all(copies, GRID, 0, 0, tiled=True).reshape(half, slots)  7.49 us
    all_to_all x1, waiting for transfers between devices, local(): x = lax.all_to_all(copies, GRID, 0, 0, tiled=True).reshape(half, slots)  5.86 us
    unnamed x8, local copies, waits for them, and re-layouts  2.76 us
  transfers between devices with their start and end apart: 3, of which 2 were waited for; matrix products, arithmetic and copies ran while one was open for 0% of the time, Pallas kernels for 12%

profile of v3, /device:TPU:2, one launch (start us, length us, event | category | flops | bytes accessed | tf_op | source)
XLA Modules:
  0.0 94.3 jit_solution(2802602676170014660)
XLA Ops:
  0.0 1.7 %shard_map.64 = (bf16[256,96]{1,0:T(8,128)(2,1)}, f32[256,32]{1,0:T(8,128)}) custom-call(bf16[32,96]{1,0:T(8,128)(2,1)} %tokens_far.1, s32[4,32]{1,0:T(4,128)} %bitcast.26, s32[4,32]{1,0:T(4,128)} %bitcast.27), custom_call_target="tpu_custom_call" | custom-call | bytes 81920 | tf_op jit(solution)/shard_map/pallas_call | solution.py:33
  1.7 15.2 %all-to-all-start = ((bf16[16,16,96]{2,1,0:T(8,128)(2,1)}), bf16[16,16,96]{2,1,0:T(8,128)(2,1)S(1)}, u32[]{:S(2)}, u32[]{:S(2)}) async-start(bf16[16,16,96]{2,1,0:T(8,128)(2,1)} %bitcast.25), calls=%async_computation | async-start | bytes 131072 | tf_op jit(solution)/shard_map/all_to_all | solution.py:209
  16.9 4.2 %shard_map.65._ = bf16[3,168,1536]{2,1,0:T(8,128)(2,1)} custom-call(s32[1]{0:T(128)} %bitcast.4.core_ref, bf16[168,3072]{1,0:T(8,128)(2,1)} %bitcast.19, bf16[168,3072]{1,0:T(8,128)(2,1)} %bitcast.21, bf16[168,3072]{1,0:T(8,128)(2,1)} %bitcast.23, bf16[256,96]{1,0:T(8,128)(2,1)} %get-tuple-element.12._), custom_call_target="tpu_custom_call" | custom-call | flops 1189085184 | bytes 1548288 | tf_op jit(solution)/shard_map/pallas_call | solution.py:33
  21.2 8.5 %all-to-all-done = bf16[16,16,96]{2,1,0:T(8,128)(2,1)S(1)} async-done(((bf16[16,16,96]{2,1,0:T(8,128)(2,1)}), bf16[16,16,96]{2,1,0:T(8,128)(2,1)S(1)}, u32[]{:S(2)}, u32[]{:S(2)}) %all-to-all-start) | async-done | bytes 49184 | tf_op jit(solution)/shard_map/all_to_all | solution.py:209
  29.7 1.1 %shard_map.66 = (bf16[16,96,256]{2,1,0:T(8,128)(2,1)}, bf16[3,168,1536]{2,1,0:T(8,128)(2,1)}) custom-call(bf16[256,96]{1,0:T(8,128)(2,1)S(1)} %bitcast.16, bf16[3,168,1536]{2,1,0:T(8,128)(2,1)} %shard_map.65._), custom_call_target="tpu_custom_call", output_to_operand_aliasing={{1}: (1, {})} | custom-call | bytes 2383872 | tf_op jit(solution)/shard_map/pallas_call | solution.py:33
  30.8 1.9 %collective-permute-start = (bf16[3,168,1536]{2,1,0:T(8,128)(2,1)}, bf16[3,168,1536]{2,1,0:T(8,128)(2,1)S(1)}, u32[]{:S(2)}, u32[]{:S(2)}) collective-permute-start(bf16[3,168,1536]{2,1,0:T(8,128)(2,1)} %get-tuple-element.14), channel_id=1, source_target_pairs={{0,1},{1,0},{2,3},{3,2},{4,5},{5,4},{6,7},{7,6},{8,9},{9,8},{10,11... | collective-permute-start | bytes 4644872 | tf_op jit(solution)/shard_map/ppermute | solution.py:234
  32.7 7.5 %all-to-all-start.1 = ((bf16[16,96,256]{2,1,0:T(8,128)(2,1)}), bf16[16,96,256]{2,1,0:T(8,128)(2,1)S(1)}, u32[]{:S(2)}, u32[]{:S(2)}) async-start(bf16[16,96,256]{2,1,0:T(8,128)(2,1)} %get-tuple-element.13), calls=%async_computation.1 | async-start | bytes 1572864 | tf_op jit(solution)/shard_map/all_to_all | solution.py:247
  40.2 0.0 collective-permute-done.got_far
  40.2 0.0 copy-start.3
  40.2 1.1 %copy-done.3 = bf16[3,168,1536]{2,1,0:T(8,128)(2,1)} copy-done((bf16[3,168,1536]{2,1,0:T(8,128)(2,1)}, bf16[3,168,1536]{2,1,0:T(8,128)(2,1)S(1)}, u32[]{:S(2)}) %copy-start.3) | copy-done | bytes 1548312
  41.3 6.7 %shard_map.67 = (bf16[4,176,1536]{2,1,0:T(8,128)(2,1)}, bf16[2,1536,168]{2,1,0:T(8,128)(2,1)}) custom-call(s32[1]{0:T(128)} %bitcast.4.core_ref, bf16[168,3072]{1,0:T(8,128)(2,1)} %bitcast.20, bf16[168,3072]{1,0:T(8,128)(2,1)} %bitcast.22, bf16[168,3072]{1,0:T(8,128)(2,1)} %bitcast.24, bf16[3,168,1536]{2,1,0:T(8,128)(2,1)} %copy-done.3), custom_call_target="tpu_custom_call" | custom-call | tf_op jit(solution)/shard_map/pallas_call | solution.py:33
  48.0 5.9 %all-to-all-done.1 = bf16[16,96,256]{2,1,0:T(8,128)(2,1)S(1)} async-done(((bf16[16,96,256]{2,1,0:T(8,128)(2,1)}), bf16[16,96,256]{2,1,0:T(8,128)(2,1)S(1)}, u32[]{:S(2)}, u32[]{:S(2)}) %all-to-all-start.1) | async-done | bytes 786464 | tf_op jit(solution)/shard_map/all_to_all | solution.py:247
  53.9 0.0 copy-start
  53.9 1.6 %copy-done = bf16[4,176,1536]{2,1,0:T(8,128)(2,1)S(1)} copy-done((bf16[4,176,1536]{2,1,0:T(8,128)(2,1)S(1)}, bf16[4,176,1536]{2,1,0:T(8,128)(2,1)}, u32[]{:S(2)}) %copy-start) | copy-done | bytes 2162712
  55.5 0.0 copy-start.1
  55.5 0.7 shard_map.68
  56.2 2.3 %all_gather.3.halves_ref = bf16[8,168,256]{2,1,0:T(8,128)(2,1)S(1)} all-gather(bf16[4,168,256]{2,1,0:T(8,128)(2,1)S(1)} %shard_map.68), channel_id=1, replica_groups=mesh['expert'=16,'y'=4,'x'=4,'core'=2] {'core'}, dimensions={0}, use_global_device_ids=true | all-gather | bytes 1032192 | tf_op jit(solution)/shard_map/all_gather | solution.py:254
  58.5 0.0 copy-done.1
  58.5 0.6 shard_map.69
  59.1 0.0 copy-start.2
  59.2 17.8 %all_to_all.20.pieces_ref = bf16[16,96,256]{2,1,0:T(8,128)(2,1)S(1)} all-to-all(bf16[16,96,256]{2,1,0:T(8,128)(2,1)S(1)} %bitcast.14), channel_id=1, replica_groups=mesh['expert'=16,'y'=4,'x'=4,'core'=2] {'y','x'}, dimensions={0} | all-to-all | bytes 1572864 | tf_op jit(solution)/shard_map/all_to_all | solution.py:256
  77.0 0.3 shard_map.70
  77.3 16.2 %all_to_all.21 = bf16[16,16,96]{2,1,0:T(8,128)(2,1)S(1)} all-to-all(bf16[16,16,96]{2,1,0:T(8,128)(2,1)S(1)} %bitcast.18), channel_id=1, replica_groups=mesh['expert'=16,'y'=4,'x'=4,'core'=2] {'expert'}, dimensions={0} | all-to-all | bytes 98304 | tf_op jit(solution)/shard_map/all_to_all | solution.py:258
  93.5 0.0 copy-done.2
  93.5 0.8 shard_map.71
Async XLA Ops:
  1.7 27.9 %all-to-all-start = ((bf16[16,16,96]{2,1,0:T(8,128)(2,1)}), bf16[16,16,96]{2,1,0:T(8,128)(2,1)S(1)}, u32[]{:S(2)}, u32[]{:S(2)}) async-start(bf16[16,16,96]{2,1,0:T(8,128)(2,1)} %bitcast.25), calls=%async_computation | async-start | bytes 131072 | tf_op jit(solution)/shard_map/all_to_all | solution.py:209
  30.8 9.4 %collective-permute-start = (bf16[3,168,1536]{2,1,0:T(8,128)(2,1)}, bf16[3,168,1536]{2,1,0:T(8,128)(2,1)S(1)}, u32[]{:S(2)}, u32[]{:S(2)}) collective-permute-start(bf16[3,168,1536]{2,1,0:T(8,128)(2,1)} %get-tuple-element.14), channel_id=1, source_target_pairs={{0,1},{1,0},{2,3},{3,2},{4,5},{5,4},{6,7},{7,6},{8,9},{9,8},{10,11... | collective-permute-start | bytes 4644872 | tf_op jit(solution)/shard_map/ppermute | solution.py:234
  32.7 21.2 %all-to-all-start.1 = ((bf16[16,96,256]{2,1,0:T(8,128)(2,1)}), bf16[16,96,256]{2,1,0:T(8,128)(2,1)S(1)}, u32[]{:S(2)}, u32[]{:S(2)}) async-start(bf16[16,96,256]{2,1,0:T(8,128)(2,1)} %get-tuple-element.13), calls=%async_computation.1 | async-start | bytes 1572864 | tf_op jit(solution)/shard_map/all_to_all | solution.py:247
  40.2 1.2 %copy-start.3 = (bf16[3,168,1536]{2,1,0:T(8,128)(2,1)}, bf16[3,168,1536]{2,1,0:T(8,128)(2,1)S(1)}, u32[]{:S(2)}) copy-start(bf16[3,168,1536]{2,1,0:T(8,128)(2,1)S(1)} %collective-permute-done.got_far) | copy-start | bytes 4644868
  53.9 1.6 %copy-start = (bf16[4,176,1536]{2,1,0:T(8,128)(2,1)S(1)}, bf16[4,176,1536]{2,1,0:T(8,128)(2,1)}, u32[]{:S(2)}) copy-start(bf16[4,176,1536]{2,1,0:T(8,128)(2,1)} %get-tuple-element.15) | copy-start | bytes 6488068
  55.5 3.0 %copy-start.1 = (bf16[2,1536,168]{2,1,0:T(8,128)(2,1)S(1)}, bf16[2,1536,168]{2,1,0:T(8,128)(2,1)}, u32[]{:S(2)}) copy-start(bf16[2,1536,168]{2,1,0:T(8,128)(2,1)} %get-tuple-element.16.fall_ref) | copy-start | bytes 3096580
  59.1 34.3 %copy-start.2 = (f32[256,32]{1,0:T(8,128)S(1)}, f32[256,32]{1,0:T(8,128)}, u32[]{:S(2)}) copy-start(f32[256,32]{1,0:T(8,128)} %get-tuple-element.11.mix_ref) | copy-start | bytes 98308

commit v4 on v3

--- a/solution.py
+++ b/solution.py
@@ -24,7 +24,7 @@
     return same.astype(F32).astype(BF16)
 
 
-def call(body, out, operands, flops=0, core=None, far=(), aliases={}, far_out=0, scratch=(), cost=True, grant=20480):
+def call(body, out, operands, flops=0, core=None, far=(), far_out=0, scratch=(), grant=20480):
     scalar = () if core is None else (core,)
     specs = [pl.BlockSpec(memory_space=pltpu.SMEM)] * len(scalar) + [VMEM] * len(operands) + [ANY] * len(far)
     outs = jax.tree.leaves(out)
@@ -35,10 +35,9 @@
         out_shape=out,
         in_specs=specs,
         out_specs=tuple(out_specs) if isinstance(out, tuple) else out_specs[0],
-        input_output_aliases=aliases,
         scratch_shapes=list(scratch),
         compiler_params=pltpu.CompilerParams(vmem_limit_bytes=grant * 2**10),
-        cost_estimate=pl.CostEstimate(flops=flops * cost, bytes_accessed=moved * cost, transcendentals=0),
+        cost_estimate=pl.CostEstimate(flops=flops, bytes_accessed=moved, transcendentals=0),
     )(*scalar, *operands, *far)
 
 
@@ -74,30 +73,28 @@
     placed_ref[...] = dot(dispatch, tokens_ref[...], ((1,), (0,))).astype(BF16)
 
 
-def turn_kernel(arrived_ref, _, copies_ref, __):
+def turn_kernel(arrived_ref, copies_ref):
     n, depth, _ = copies_ref.shape
     turned = dot(eye(depth), arrived_ref[...], ((1,), (1,))).astype(BF16)
     for i in range(n):
         copies_ref[i] = turned
 
 
-def picker(depth, group, which):
-    wide, thin = 2 * group * depth, group * depth
-    source = lax.broadcasted_iota(jnp.int32, (wide, thin), 0)
-    target = lax.broadcasted_iota(jnp.int32, (wide, thin), 1)
-    return (source == target + (target // depth + which) * depth).astype(F32).astype(BF16)
-
-
 def pick_kernel(depth, core_ref, gate_far, up_far, down_far, _, send_far, weights_ref, send_ref, sems, out_sems):
     loads = fetch([(far, weights_ref.at[k]) for k, far in enumerate((gate_far, up_far, down_far))], sems)
     wide, thin = 8 * depth, 4 * depth
-    pick = picker(depth, 4, 1 - core_ref[0])
     stores = []
     for k, load in enumerate(loads):
         load.wait()
-        for g in range(weights_ref.shape[2] // wide):
-            block = weights_ref[k, :, g * wide : (g + 1) * wide]
-            send_ref[k, :, g * thin : (g + 1) * thin] = dot(block, pick, ((1,), (0,))).astype(BF16)
+        for which in range(2):
+
+            @pl.when(core_ref[0] != which)
+            def _():
+                for g in range(weights_ref.shape[2] // wide):
+                    starts = [g * wide + (2 * i + which) * depth for i in range(4)]
+                    pieces = [weights_ref[k, :, start : start + depth] for start in starts]
+                    send_ref[k, :, g * thin : (g + 1) * thin] = jnp.concatenate(pieces, axis=1)
+
         store = pltpu.make_async_copy(send_ref.at[k], send_far.at[k], out_sems.at[k])
         store.start()
         stores.append(store)
@@ -105,60 +102,35 @@
         store.wait()
 
 
-def stack_kernel(
-    depth, core_ref, gate_far, up_far, down_far, got_far, rise_ref, fall_far, weights_ref, got_ref, fall_ref, sems
-):
-    pairs = [(far, weights_ref.at[k]) for k, far in enumerate((gate_far, up_far, down_far))]
-    loads = fetch(pairs + [(got_far.at[k], got_ref.at[k]) for k in range(3)], sems)
-    units = got_ref.shape[1]
-    pad = rise_ref.shape[1] - units
-    wide, thin = 8 * depth, 4 * depth
+def rise_kernel(core_ref, x_ref, gate_ref, up_ref, got_ref, out_ref, spread_ref):
     own, other = core_ref[0], 1 - core_ref[0]
-    pick = picker(depth, 4, own)
-    for k in range(4):
-        rise_ref[k, units:] = jnp.zeros((pad, rise_ref.shape[2]), BF16)
-    stores = [pltpu.make_async_copy(fall_ref.at[u], fall_far.at[u], sems.at[6 + i]) for i, u in enumerate((own, other))]
-    for k in reversed(range(3)):
-        loads[k].wait()
-        for g in range(weights_ref.shape[2] // wide):
-            block = weights_ref[k, :, g * wide : (g + 1) * wide]
-            chosen = dot(block, pick, ((1,), (0,))).astype(BF16)
-            if k < 2:
-                rise_ref[2 * own + k, :units, g * thin : (g + 1) * thin] = chosen
-            else:
-                fall_ref[own, g * thin : (g + 1) * thin] = chosen.T
-        if k == 2:
-            stores[0].start()
-    for k in reversed(range(3)):
-        loads[3 + k].wait()
-        if k < 2:
-            rise_ref[2 * other + k, :units] = got_ref[k]
-        else:
-            fall_ref[other] = got_ref[k].T
-            stores[1].start()
-    for store in stores:
-        store.wait()
-
-
-def rise_kernel(x_ref, rise_ref, out_ref):
-    n, units, slots = out_ref.shape
-    padded = rise_ref.shape[0] // n
-    product = dot(rise_ref[...], x_ref[...], ((1,), (0,)))
-    for k in range(n):
-        out_ref[k] = product[k * padded : k * padded + units].astype(BF16)
-
-
-def fall_kernel(halves_ref, fall_ref, out_ref):
+    n, depth, _ = x_ref.shape
+    for i in range(n):
+        spread_ref[pl.ds(pl.multiple_of((2 * i + own) * depth, depth), depth)] = x_ref[i]
+        spread_ref[pl.ds(pl.multiple_of((2 * i + other) * depth, depth), depth)] = jnp.zeros_like(x_ref[i])
+    x = x_ref[...].reshape(n * depth, x_ref.shape[2])
+    for k, ref in enumerate((gate_ref, up_ref)):
+        out_ref[2 * own + k] = dot(ref[...], spread_ref[...], ((1,), (0,))).astype(BF16)
+        out_ref[2 * other + k] = dot(got_ref[k], x, ((1,), (0,))).astype(BF16)
+
+
+def fall_kernel(core_ref, halves_ref, down_ref, got_ref, out_ref, part_ref):
+    own, other = core_ref[0], 1 - core_ref[0]
+    n, depth, _ = out_ref.shape
     hidden = []
-    for u in range(2):
+    for u in (own, other):
         gate = halves_ref[2 * u].astype(F32) + halves_ref[4 + 2 * u].astype(F32)
         up = halves_ref[2 * u + 1].astype(F32) + halves_ref[5 + 2 * u].astype(F32)
         hidden.append((gate / (1.0 + jnp.exp(-gate)) * up).astype(BF16))
-    chunk = 384
-    for i in range(out_ref.shape[0] // chunk):
-        at = slice(i * chunk, (i + 1) * chunk)
-        part = dot(fall_ref[0, at], hidden[0], ((1,), (0,))) + dot(fall_ref[1, at], hidden[1], ((1,), (0,)))
-        out_ref[at] = part.astype(BF16)
+    part_ref[...] = dot(down_ref[...], hidden[0], ((0,), (0,)))
+    group = 4
+    for g in range(n // group):
+        columns = slice(g * group * depth, (g + 1) * group * depth)
+        rest = dot(got_ref[2, :, columns], hidden[1], ((0,), (0,)))
+        for j in range(group):
+            i = g * group + j
+            first = part_ref[pl.ds(pl.multiple_of((2 * i + own) * depth, depth), depth)]
+            out_ref[i] = (first + rest[j * depth : (j + 1) * depth]).astype(BF16)
 
 
 def sum_kernel(pieces_ref, out_ref):
@@ -211,49 +183,38 @@
     weights = (w_gate[0], w_up[0], w_down[0])
     thirds = shape(3, units, half)
     whole_ref, third_ref = pltpu.VMEM((3, units, width), BF16), pltpu.VMEM(thirds.shape, BF16)
-    picking = 3 * 2 * units * half * 8 * depth
     send = call(
         functools.partial(pick_kernel, depth),
         thirds,
         (),
-        flops=picking,
+        flops=10**8,
         core=core,
         far=(*weights, placed),
         far_out=1,
         scratch=(whole_ref, third_ref, pltpu.SemaphoreType.DMA((3,)), pltpu.SemaphoreType.DMA((3,))),
         grant=65024,
     )
-    copies, send = call(
-        turn_kernel,
-        (shape(chips, depth, slots), thirds),
-        (arrived.reshape(slots, depth),),
-        far=(send,),
-        aliases={1: 1},
-        far_out=1,
-    )
     got = lax.ppermute(send, "core", ((0, 1), (1, 0)))
-    rise, fall = call(
-        functools.partial(stack_kernel, depth),
-        (shape(4, padded, half), shape(2, half, units)),
-        (),
-        core=core,
-        far=(*weights, got),
-        far_out=1,
-        scratch=(whole_ref, third_ref, pltpu.VMEM((2, half, units), BF16), pltpu.SemaphoreType.DMA((8,))),
-        cost=False,
-        grant=61440,
-    )
-
-    x = lax.all_to_all(copies, GRID, 0, 0, tiled=True).reshape(half, slots)
+    copies = call(turn_kernel, shape(chips, depth, slots), (arrived.reshape(slots, depth),), flops=10**11)
+    x = lax.all_to_all(copies, GRID, 0, 0, tiled=True)
     partial = call(
         rise_kernel,
         shape(4, units, slots),
-        (x, rise.reshape(4 * padded, half)),
-        flops=2 * 4 * padded * half * slots,
+        (x, *weights[:2], got),
+        flops=2 * 6 * units * half * slots,
+        core=core,
+        scratch=(pltpu.VMEM((width, slots), BF16),),
     )
     halves = lax.all_gather(partial, "core", axis=0, tiled=True)
-    part = call(fall_kernel, shape(half, slots), (halves, fall), flops=2 * 2 * units * half * slots)
-    pieces = lax.all_to_all(part.reshape(chips, depth, slots), GRID, 0, 0, tiled=True)
+    part = call(
+        fall_kernel,
+        shape(chips, depth, slots),
+        (halves, weights[2], got),
+        flops=2 * 3 * units * half * slots,
+        core=core,
+        scratch=(pltpu.VMEM((width, slots), F32),),
+    )
+    pieces = lax.all_to_all(part, GRID, 0, 0, tiled=True)
     summed = call(sum_kernel, shape(slots, depth), (pieces,))
     returned = lax.all_to_all(summed.reshape(experts, capacity, depth), "expert", 0, 0, tiled=True)
     return call(mix_kernel, shape(rows, depth), (mix, returned.reshape(slots, depth)))

time: 94.8 us -> 91.7 us (0.967)
  blocking collectives: 36.3 us -> 58.1 us
  Pallas kernels: 16.2 us -> 8.18 us
  starting transfers between devices: 24.6 us -> 17.1 us
  waiting for transfers between devices: 14.3 us -> 7.77 us
  local copies, waits for them, and re-layouts: 2.76 us -> 0.02 us
    all_to_all x1 -> x2, blocking collectives: 17.8 us -> 36.7 us  [the longest x1 19 us: local(): x = lax.all_to_all(copies, GRID, 0, 0, tiled=True)]
    pallas_call x8 -> x7, Pallas kernels: 16.2 us -> 8.18 us  [call(): pl.pallas_call(body, out_shape=out, in_specs=specs, out_specs=tuple(out_s...]
    all_to_all x1 -> x0, starting transfers between devices: 7.49 us -> none  [local(): x = lax.all_to_all(copies, GRID, 0, 0, tiled=True).reshape(half, slots)]
    all_to_all x1 -> x0, waiting for transfers between devices: 5.86 us -> none  [local(): x = lax.all_to_all(copies, GRID, 0, 0, tiled=True).reshape(half, slots)]
    all_to_all x1, blocking collectives: 16.2 us -> 19 us  [local(): lax.all_to_all(summed.reshape(experts, capacity, depth), 'expert', 0, 0,...]
    unnamed x8, local copies, waits for them, and re-layouts: 2.76 us -> 0.02 us
  transfers between devices with their start and end apart: 3 -> 2, of which waited for: 2 -> 1; matrix products, arithmetic and copies ran while one was open for 0% -> 0% of each run, Pallas kernels for 12% -> 4%
where the time goes in v4:
time: 91.7 us; the launch traced here: 91.3 us
  blocking collectives  58.1 us (63%)
  starting transfers between devices  17.1 us (19%)
  Pallas kernels  8.18 us (9%)
  waiting for transfers between devices  7.77 us (8%)
    all_to_all x1, blocking collectives, local(): x = lax.all_to_all(copies, GRID, 0, 0, tiled=True)  19 us
    all_to_all x1, blocking collectives, local(): lax.all_to_all(summed.reshape(experts, capacity, depth), 'expert', 0, 0,...  19 us
    all_to_all x1, blocking collectives, local(): pieces = lax.all_to_all(part, GRID, 0, 0, tiled=True)  17.7 us
    all_to_all x1, starting transfers between devices, local(): lax.all_to_all(placed.reshape(experts, capacity, depth), 'expert', 0, 0,...  15.2 us
    pallas_call x7, Pallas kernels, call(): pl.pallas_call(body, out_shape=out, in_specs=specs, out_specs=tuple(out_s...  8.18 us
    all_to_all x1, waiting for transfers between devices, local(): lax.all_to_all(placed.reshape(experts, capacity, depth), 'expert', 0, 0,...  7.77 us
    all_gather x1, blocking collectives, local(): halves = lax.all_gather(partial, 'core', axis=0, tiled=True)  2.43 us
    ppermute x1, starting transfers between devices, local(): got = lax.ppermute(send, 'core', ((0, 1), (1, 0)))  1.92 us
  transfers between devices with their start and end apart: 2, of which 1 were waited for; matrix products, arithmetic and copies ran while one was open for 0% of the time, Pallas kernels for 4%

profile of v4, /device:TPU:2, one launch (start us, length us, event | category | flops | bytes accessed | tf_op | source)
XLA Modules:
  0.0 91.3 jit_solution(12215794536409764233)
XLA Ops:
  0.0 1.7 %shard_map.64 = (bf16[256,96]{1,0:T(8,128)(2,1)}, f32[256,32]{1,0:T(8,128)}) custom-call(bf16[32,96]{1,0:T(8,128)(2,1)} %tokens_far.1, s32[4,32]{1,0:T(4,128)} %bitcast.20, s32[4,32]{1,0:T(4,128)} %bitcast.21), custom_call_target="tpu_custom_call" | custom-call | bytes 81920 | tf_op jit(solution)/shard_map/pallas_call | solution.py:33
  1.7 15.2 %all-to-all-start = ((bf16[16,16,96]{2,1,0:T(8,128)(2,1)}), bf16[16,16,96]{2,1,0:T(8,128)(2,1)S(1)}, u32[]{:S(2)}, u32[]{:S(2)}) async-start(bf16[16,16,96]{2,1,0:T(8,128)(2,1)} %bitcast.19), calls=%async_computation | async-start | bytes 131072 | tf_op jit(solution)/shard_map/all_to_all | solution.py:181
  16.9 3.0 %shard_map.66 = bf16[3,168,1536]{2,1,0:T(8,128)(2,1)} custom-call(s32[1]{0:T(128)} %bitcast.2.core_ref, bf16[168,3072]{1,0:T(8,128)(2,1)} %bitcast.10, bf16[168,3072]{1,0:T(8,128)(2,1)} %bitcast.12, bf16[168,3072]{1,0:T(8,128)(2,1)} %bitcast.14, bf16[256,96]{1,0:T(8,128)(2,1)} %get-tuple-element.8._), custom_call_target="tpu_custom_call" | custom-call | flops 100000000 | bytes 1548288 | tf_op jit(solution)/shard_map/pallas_call | solution.py:33
  19.9 1.9 %collective-permute-start = (bf16[3,168,1536]{2,1,0:T(8,128)(2,1)}, bf16[3,168,1536]{2,1,0:T(8,128)(2,1)S(1)}, u32[]{:S(2)}, u32[]{:S(2)}) collective-permute-start(bf16[3,168,1536]{2,1,0:T(8,128)(2,1)} %shard_map.66), channel_id=1, source_target_pairs={{0,1},{1,0},{2,3},{3,2},{4,5},{5,4},{6,7},{7,6},{8,9},{9,8},{10,11... | collective-permute-start | bytes 4644872 | tf_op jit(solution)/shard_map/ppermute | solution.py:197
  21.9 7.8 %all-to-all-done = bf16[16,16,96]{2,1,0:T(8,128)(2,1)S(1)} async-done(((bf16[16,16,96]{2,1,0:T(8,128)(2,1)}), bf16[16,16,96]{2,1,0:T(8,128)(2,1)S(1)}, u32[]{:S(2)}, u32[]{:S(2)}) %all-to-all-start) | async-done | bytes 49184 | tf_op jit(solution)/shard_map/all_to_all | solution.py:181
  29.6 0.0 copy-start.1
  29.6 0.2 shard_map.65
  29.9 0.0 copy-start
  29.9 19.0 %all_to_all.20.x_ref = bf16[16,96,256]{2,1,0:T(8,128)(2,1)S(1)} all-to-all(bf16[16,96,256]{2,1,0:T(8,128)(2,1)S(1)} %shard_map.65), channel_id=1, replica_groups=mesh['expert'=16,'y'=4,'x'=4,'core'=2] {'y','x'}, dimensions={0} | all-to-all | bytes 1572864 | tf_op jit(solution)/shard_map/all_to_all | solution.py:199
  48.9 0.0 collective-permute-done.got_ref
  48.9 0.0 copy-done.1
  48.9 0.0 copy-done
  48.9 1.1 %shard_map.67 = bf16[4,168,256]{2,1,0:T(8,128)(2,1)S(1)} custom-call(s32[1]{0:T(128)} %bitcast.2.core_ref, bf16[16,96,256]{2,1,0:T(8,128)(2,1)S(1)} %all_to_all.20.x_ref, bf16[168,3072]{1,0:T(8,128)(2,1)S(1)} %bitcast.11, bf16[168,3072]{1,0:T(8,128)(2,1)S(1)} %bitcast.13, bf16[3,168,1536]{2,1,0:T(8,128)(2,1)S(1)} %collective-permute-done.got_ref), custom_call_target="tpu_custom_call" | custom-call | flops 792723456 | bytes 4743168 | tf_op jit(solution)/shard_map/pallas_call | solution.py:33
  50.0 0.0 copy-start.2
  50.0 2.4 %all_gather.3.halves_ref = bf16[8,168,256]{2,1,0:T(8,128)(2,1)S(1)} all-gather(bf16[4,168,256]{2,1,0:T(8,128)(2,1)S(1)} %shard_map.67), channel_id=1, replica_groups=mesh['expert'=16,'y'=4,'x'=4,'core'=2] {'core'}, dimensions={0}, use_global_device_ids=true | all-gather | bytes 1032192 | tf_op jit(solution)/shard_map/all_gather | solution.py:208
  52.5 0.0 copy-done.2
  52.5 1.0 %shard_map.68 = bf16[16,96,256]{2,1,0:T(8,128)(2,1)S(1)} custom-call(s32[1]{0:T(128)} %bitcast.2.core_ref, bf16[8,168,256]{2,1,0:T(8,128)(2,1)S(1)} %all_gather.3.halves_ref, bf16[168,3072]{1,0:T(8,128)(2,1)S(1)} %bitcast.15, bf16[3,168,1536]{2,1,0:T(8,128)(2,1)S(1)} %collective-permute-done.got_ref), custom_call_target="tpu_custom_call" | custom-call | flops 396361728 | bytes 4055040 | tf_op jit(solution)/shard_map/pallas_call | solution.py:33
  53.5 0.0 copy-start.3
  53.5 17.7 %all_to_all.21.pieces_ref = bf16[16,96,256]{2,1,0:T(8,128)(2,1)S(1)} all-to-all(bf16[16,96,256]{2,1,0:T(8,128)(2,1)S(1)} %shard_map.68), channel_id=1, replica_groups=mesh['expert'=16,'y'=4,'x'=4,'core'=2] {'y','x'}, dimensions={0} | all-to-all | bytes 1572864 | tf_op jit(solution)/shard_map/all_to_all | solution.py:217
  71.2 0.3 shard_map.69
  71.5 19.0 %all_to_all.22 = bf16[16,16,96]{2,1,0:T(8,128)(2,1)S(1)} all-to-all(bf16[16,16,96]{2,1,0:T(8,128)(2,1)S(1)} %bitcast.17), channel_id=1, replica_groups=mesh['expert'=16,'y'=4,'x'=4,'core'=2] {'expert'}, dimensions={0} | all-to-all | bytes 98304 | tf_op jit(solution)/shard_map/all_to_all | solution.py:219
  90.5 0.0 copy-done.3
  90.5 0.8 shard_map.70
Async XLA Ops:
  1.7 27.9 %all-to-all-start = ((bf16[16,16,96]{2,1,0:T(8,128)(2,1)}), bf16[16,16,96]{2,1,0:T(8,128)(2,1)S(1)}, u32[]{:S(2)}, u32[]{:S(2)}) async-start(bf16[16,16,96]{2,1,0:T(8,128)(2,1)} %bitcast.19), calls=%async_computation | async-start | bytes 131072 | tf_op jit(solution)/shard_map/all_to_all | solution.py:181
  19.9 28.9 %collective-permute-start = (bf16[3,168,1536]{2,1,0:T(8,128)(2,1)}, bf16[3,168,1536]{2,1,0:T(8,128)(2,1)S(1)}, u32[]{:S(2)}, u32[]{:S(2)}) collective-permute-start(bf16[3,168,1536]{2,1,0:T(8,128)(2,1)} %shard_map.66), channel_id=1, source_target_pairs={{0,1},{1,0},{2,3},{3,2},{4,5},{5,4},{6,7},{7,6},{8,9},{9,8},{10,11... | collective-permute-start | bytes 4644872 | tf_op jit(solution)/shard_map/ppermute | solution.py:197
  29.6 19.2 %copy-start.1 = (bf16[1,168,3072]{2,1,0:T(8,128)(2,1)S(1)}, bf16[1,168,3072]{2,1,0:T(8,128)(2,1)}, u32[]{:S(2)}) copy-start(bf16[1,168,3072]{2,1,0:T(8,128)(2,1)} %param.10) | copy-start | bytes 3096580
  29.9 19.0 %copy-start = (bf16[1,168,3072]{2,1,0:T(8,128)(2,1)S(1)}, bf16[1,168,3072]{2,1,0:T(8,128)(2,1)}, u32[]{:S(2)}) copy-start(bf16[1,168,3072]{2,1,0:T(8,128)(2,1)} %param.9) | copy-start | bytes 3096580
  50.0 2.4 %copy-start.2 = (bf16[1,168,3072]{2,1,0:T(8,128)(2,1)S(1)}, bf16[1,168,3072]{2,1,0:T(8,128)(2,1)}, u32[]{:S(2)}) copy-start(bf16[1,168,3072]{2,1,0:T(8,128)(2,1)} %param.11) | copy-start | bytes 3096580
  53.5 37.0 %copy-start.3 = (f32[256,32]{1,0:T(8,128)S(1)}, f32[256,32]{1,0:T(8,128)}, u32[]{:S(2)}) copy-start(f32[256,32]{1,0:T(8,128)} %get-tuple-element.7.mix_ref) | copy-start | bytes 98308

commit v5 on v4

--- a/solution.py
+++ b/solution.py
@@ -6,13 +6,13 @@
 from jax import lax
 from jax.experimental import pallas as pl
 from jax.experimental.pallas import tpu as pltpu
-from jax.sharding import Mesh, PartitionSpec as P
-
-GRID = ("y", "x")
+from jax.sharding import PartitionSpec as P
+
 VMEM = pl.BlockSpec(memory_space=pltpu.VMEM)
 ANY = pl.BlockSpec(memory_space=pltpu.HBM)
 BF16 = jnp.bfloat16
 F32 = jnp.float32
+FIRST, LAST = 11, 8
 
 
 def dot(left, right, dims, precision=None):
@@ -22,6 +22,17 @@
 def eye(n):
     same = lax.broadcasted_iota(jnp.int32, (n, n), 0) == lax.broadcasted_iota(jnp.int32, (n, n), 1)
     return same.astype(F32).astype(BF16)
+
+
+def store_turned(ref, value, shift):
+    cut = shift % value.shape[0]
+    ref[: value.shape[0] - cut] = value[cut:]
+    if cut:
+        ref[value.shape[0] - cut :] = value[:cut]
+
+
+def chip_at(i, n):
+    return (i + n - 1) % n
 
 
 def call(body, out, operands, flops=0, core=None, far=(), far_out=0, scratch=(), grant=20480):
@@ -48,14 +59,15 @@
     return copies
 
 
-def place_kernel(capacity, tokens_far, routes_far, weight_far, placed_ref, mix_ref, tokens_ref, routes_ref, weight_ref, sems):
+def place_kernel(capacity, first, shift, tokens_far, routes_far, weight_far, placed_ref, mix_ref, tokens_ref, routes_ref, weight_ref, sems):
     pairs = ((tokens_far, tokens_ref), (routes_far, routes_ref), (weight_far, weight_ref))
     for copy in fetch(pairs, sems):
         copy.wait()
     top, rows = routes_ref.shape
     slots = placed_ref.shape[0]
     slot = lax.broadcasted_iota(jnp.int32, (slots, rows), 0)
-    expert = slot // capacity
+    experts = slots // capacity
+    expert = (slot // capacity + first) % experts
     spot = slot % capacity
     weight = weight_ref[...].astype(F32)
     share = weight / jnp.sum(weight, axis=0, keepdims=True)
@@ -68,7 +80,7 @@
     earlier = lax.broadcasted_iota(jnp.int32, (rows, rows), 0) < lax.broadcasted_iota(jnp.int32, (rows, rows), 1)
     before = dot(named.astype(BF16), earlier.astype(F32).astype(BF16), ((1,), (0,)))
     here = (named > 0.5) & (before.astype(jnp.int32) == spot)
-    mix_ref[...] = jnp.where(here, mix, 0.0)
+    store_turned(mix_ref, jnp.where(here, mix, 0.0), shift)
     dispatch = jnp.where(here, 1.0, 0.0).astype(BF16)
     placed_ref[...] = dot(dispatch, tokens_ref[...], ((1,), (0,))).astype(BF16)
 
@@ -82,7 +94,8 @@
 
 def pick_kernel(depth, core_ref, gate_far, up_far, down_far, _, send_far, weights_ref, send_ref, sems, out_sems):
     loads = fetch([(far, weights_ref.at[k]) for k, far in enumerate((gate_far, up_far, down_far))], sems)
-    wide, thin = 8 * depth, 4 * depth
+    n = weights_ref.shape[2] // (2 * depth)
+    thin = 4 * depth
     stores = []
     for k, load in enumerate(loads):
         load.wait()
@@ -90,8 +103,8 @@
 
             @pl.when(core_ref[0] != which)
             def _():
-                for g in range(weights_ref.shape[2] // wide):
-                    starts = [g * wide + (2 * i + which) * depth for i in range(4)]
+                for g in range(n // 4):
+                    starts = [(2 * chip_at(4 * g + i, n) + which) * depth for i in range(4)]
                     pieces = [weights_ref[k, :, start : start + depth] for start in starts]
                     send_ref[k, :, g * thin : (g + 1) * thin] = jnp.concatenate(pieces, axis=1)
 
@@ -106,8 +119,9 @@
     own, other = core_ref[0], 1 - core_ref[0]
     n, depth, _ = x_ref.shape
     for i in range(n):
-        spread_ref[pl.ds(pl.multiple_of((2 * i + own) * depth, depth), depth)] = x_ref[i]
-        spread_ref[pl.ds(pl.multiple_of((2 * i + other) * depth, depth), depth)] = jnp.zeros_like(x_ref[i])
+        chip = chip_at(i, n)
+        spread_ref[pl.ds(pl.multiple_of((2 * chip + own) * depth, depth), depth)] = x_ref[i]
+        spread_ref[pl.ds(pl.multiple_of((2 * chip + other) * depth, depth), depth)] = jnp.zeros_like(x_ref[i])
     x = x_ref[...].reshape(n * depth, x_ref.shape[2])
     for k, ref in enumerate((gate_ref, up_ref)):
         out_ref[2 * own + k] = dot(ref[...], spread_ref[...], ((1,), (0,))).astype(BF16)
@@ -129,16 +143,16 @@
         rest = dot(got_ref[2, :, columns], hidden[1], ((0,), (0,)))
         for j in range(group):
             i = g * group + j
-            first = part_ref[pl.ds(pl.multiple_of((2 * i + own) * depth, depth), depth)]
+            first = part_ref[pl.ds(pl.multiple_of((2 * chip_at(i, n) + own) * depth, depth), depth)]
             out_ref[i] = (first + rest[j * depth : (j + 1) * depth]).astype(BF16)
 
 
-def sum_kernel(pieces_ref, out_ref):
+def sum_kernel(shift, pieces_ref, out_ref):
     n, depth, _ = pieces_ref.shape
     total = pieces_ref[0].astype(F32)
     for i in range(1, n):
         total += pieces_ref[i].astype(F32)
-    out_ref[...] = dot(total.astype(BF16), eye(depth), ((0,), (0,))).astype(BF16)
+    store_turned(out_ref, dot(total.astype(BF16), eye(depth), ((0,), (0,))).astype(BF16), shift)
 
 
 def mix_kernel(mix_ref, returned_ref, out_ref):
@@ -153,20 +167,26 @@
 
 
 def local(tokens, routes, route_weight, w_gate, w_up, w_down):
-    experts, chips = lax.axis_size("expert"), lax.axis_size(GRID)
+    experts, chips = lax.axis_size("expert"), lax.axis_size("tensor") // 2
     rows, depth = tokens.shape
     units, width = w_gate.shape[1:]
     half = width // 2
     padded = -(-units // 16) * 16
     capacity = min(rows, 2 * rows * routes.shape[1] // experts)
     slots = experts * capacity
-    core = lax.axis_index("core").astype(jnp.int32).reshape(1)
+    first, last = FIRST * experts // 16, LAST * experts // 16
+    order_out = [[(i + first) % experts for i in range(experts)]]
+    order_back = [[(i + last) % experts for i in range(experts)]]
+    shift = (last - first) * capacity
+    same_core = [[2 * chip_at(i, chips) + c for i in range(chips)] for c in range(2)]
+    same_chip = [[2 * i, 2 * i + 1] for i in range(chips)]
+    core = (lax.axis_index("tensor") % 2).astype(jnp.int32).reshape(1)
 
     def shape(*dims, dtype=BF16):
         return jax.ShapeDtypeStruct(dims, dtype)
 
     placed, mix = call(
-        functools.partial(place_kernel, capacity),
+        functools.partial(place_kernel, capacity, first, shift),
         (shape(slots, depth), shape(slots, rows, dtype=F32)),
         (),
         far=(tokens, routes.T, route_weight.T),
@@ -178,7 +198,7 @@
         ),
         grant=65536,
     )
-    arrived = lax.all_to_all(placed.reshape(experts, capacity, depth), "expert", 0, 0, tiled=True)
+    arrived = lax.all_to_all(placed.reshape(experts, capacity, depth), "expert", 0, 0, axis_index_groups=order_out, tiled=True)
 
     weights = (w_gate[0], w_up[0], w_down[0])
     thirds = shape(3, units, half)
@@ -194,9 +214,9 @@
         scratch=(whole_ref, third_ref, pltpu.SemaphoreType.DMA((3,)), pltpu.SemaphoreType.DMA((3,))),
         grant=65024,
     )
-    got = lax.ppermute(send, "core", ((0, 1), (1, 0)))
+    got = lax.ppermute(send, "tensor", [(i, i ^ 1) for i in range(2 * chips)])
     copies = call(turn_kernel, shape(chips, depth, slots), (arrived.reshape(slots, depth),), flops=10**11)
-    x = lax.all_to_all(copies, GRID, 0, 0, tiled=True)
+    x = lax.all_to_all(copies, "tensor", 0, 0, axis_index_groups=same_core, tiled=True)
     partial = call(
         rise_kernel,
         shape(4, units, slots),
@@ -205,7 +225,7 @@
         core=core,
         scratch=(pltpu.VMEM((width, slots), BF16),),
     )
-    halves = lax.all_gather(partial, "core", axis=0, tiled=True)
+    halves = lax.all_gather(partial, "tensor", axis=0, axis_index_groups=same_chip, tiled=True)
     part = call(
         fall_kernel,
         shape(chips, depth, slots),
@@ -214,23 +234,19 @@
         core=core,
         scratch=(pltpu.VMEM((width, slots), F32),),
     )
-    pieces = lax.all_to_all(part, GRID, 0, 0, tiled=True)
-    summed = call(sum_kernel, shape(slots, depth), (pieces,))
-    returned = lax.all_to_all(summed.reshape(experts, capacity, depth), "expert", 0, 0, tiled=True)
+    pieces = lax.all_to_all(part, "tensor", 0, 0, axis_index_groups=same_core, tiled=True)
+    summed = call(functools.partial(sum_kernel, shift), shape(slots, depth), (pieces,))
+    returned = lax.all_to_all(summed.reshape(experts, capacity, depth), "expert", 0, 0, axis_index_groups=order_back, tiled=True)
     return call(mix_kernel, shape(rows, depth), (mix, returned.reshape(slots, depth)))
 
 
 def solution(mesh):
-    chips_y = chips_x = 4
-    devices = mesh.devices
-    fine = Mesh(devices.reshape(devices.shape[0], chips_y, chips_x, 2), ("expert", "y", "x", "core"))
-    tensor = ("y", "x", "core")
     placed = (
-        P("expert", tensor),
+        P("expert", "tensor"),
         P("expert", None),
         P("expert", None),
-        P("expert", tensor, None),
-        P("expert", tensor, None),
-        P("expert", tensor, None),
-    )
-    return jax.shard_map(local, mesh=fine, in_specs=placed, out_specs=P("expert", tensor), check_vma=False)
+        P("expert", "tensor", None),
+        P("expert", "tensor", None),
+        P("expert", "tensor", None),
+    )
+    return jax.shard_map(local, mesh=mesh, in_specs=placed, out_specs=P("expert", "tensor"), check_vma=False)

time: 91.7 us -> 82.1 us (0.90)
  waiting for transfers between devices: 7.77 us -> 1.47 us
  blocking collectives: 58.1 us -> 53.7 us
  starting transfers between devices: 17.1 us -> 18.1 us
    all_to_all x1, waiting for transfers between devices: 7.77 us -> 1.46 us  [local(): lax.all_to_all(placed.reshape(experts, capacity, depth), 'expert', 0, 0,...]
    all_to_all x1, blocking collectives: 19 us -> 15.5 us  [local(): lax.all_to_all(summed.reshape(experts, capacity, depth), 'expert', 0, 0,...]
    all_to_all x1, starting transfers between devices: 15.2 us -> 16.2 us  [local(): lax.all_to_all(placed.reshape(experts, capacity, depth), 'expert', 0, 0,...]
    all_to_all x2, blocking collectives: 36.7 us -> 35.7 us  [the longest x1 18 us: local(): lax.all_to_all(part, 'tensor', 0, 0, axis_index_groups=same_core, tiled=T...]
where the time goes in v5:
time: 82.1 us; the launch traced here: 81.5 us
  blocking collectives  53.7 us (65%)
  starting transfers between devices  18.1 us (22%)
  Pallas kernels  8.17 us (10%)
  waiting for transfers between devices  1.47 us (2%)
    all_to_all x1, blocking collectives, local(): lax.all_to_all(part, 'tensor', 0, 0, axis_index_groups=same_core, tiled=T...  18 us
    all_to_all x1, blocking collectives, local(): lax.all_to_all(copies, 'tensor', 0, 0, axis_index_groups=same_core, tiled...  17.7 us
    all_to_all x1, starting transfers between devices, local(): lax.all_to_all(placed.reshape(experts, capacity, depth), 'expert', 0, 0,...  16.2 us
    all_to_all x1, blocking collectives, local(): lax.all_to_all(summed.reshape(experts, capacity, depth), 'expert', 0, 0,...  15.5 us
    pallas_call x7, Pallas kernels, call(): pl.pallas_call(body, out_shape=out, in_specs=specs, out_specs=tuple(out_s...  8.17 us
    all_gather x1, blocking collectives, local(): lax.all_gather(partial, 'tensor', axis=0, axis_index_groups=same_chip, ti...  2.43 us
    ppermute x1, starting transfers between devices, local(): got = lax.ppermute(send, 'tensor', [(i, i ^ 1) for i in range(2 * chips)])  1.92 us
  transfers between devices with their start and end apart: 2, of which 1 were waited for; matrix products, arithmetic and copies ran while one was open for 0% of the time, Pallas kernels for 4%

profile of v5, /device:TPU:2, one launch (start us, length us, event | category | flops | bytes accessed | tf_op | source)
XLA Modules:
  0.0 81.5 jit_solution(10988145329906759924)
XLA Ops:
  0.0 1.7 %shard_map.64 = (bf16[256,96]{1,0:T(8,128)(2,1)}, f32[256,32]{1,0:T(8,128)}) custom-call(bf16[32,96]{1,0:T(8,128)(2,1)} %tokens_far.1, s32[4,32]{1,0:T(4,128)} %bitcast.20, s32[4,32]{1,0:T(4,128)} %bitcast.21), custom_call_target="tpu_custom_call" | custom-call | bytes 81920 | tf_op jit(solution)/shard_map/pallas_call | solution.py:44
  1.7 16.2 %all-to-all-start = ((bf16[16,16,96]{2,1,0:T(8,128)(2,1)}), bf16[16,16,96]{2,1,0:T(8,128)(2,1)S(1)}, u32[]{:S(2)}, u32[]{:S(2)}) async-start(bf16[16,16,96]{2,1,0:T(8,128)(2,1)} %bitcast.19), calls=%async_computation | async-start | bytes 131072 | tf_op jit(solution)/shard_map/all_to_all | solution.py:201
  17.9 3.0 %shard_map.66 = bf16[3,168,1536]{2,1,0:T(8,128)(2,1)} custom-call(s32[1]{0:T(128)} %bitcast.2.core_ref, bf16[168,3072]{1,0:T(8,128)(2,1)} %bitcast.10, bf16[168,3072]{1,0:T(8,128)(2,1)} %bitcast.12, bf16[168,3072]{1,0:T(8,128)(2,1)} %bitcast.14, bf16[256,96]{1,0:T(8,128)(2,1)} %get-tuple-element.8._), custom_call_target="tpu_custom_call" | custom-call | flops 100000000 | bytes 1548288 | tf_op jit(solution)/shard_map/pallas_call | solution.py:44
  20.9 1.9 %collective-permute-start = (bf16[3,168,1536]{2,1,0:T(8,128)(2,1)}, bf16[3,168,1536]{2,1,0:T(8,128)(2,1)S(1)}, u32[]{:S(2)}, u32[]{:S(2)}) collective-permute-start(bf16[3,168,1536]{2,1,0:T(8,128)(2,1)} %shard_map.66), channel_id=1, source_target_pairs={{0,1},{1,0},{2,3},{3,2},{4,5},{5,4},{6,7},{7,6},{8,9},{9,8},{10,11... | collective-permute-start | bytes 4644872 | tf_op jit(solution)/shard_map/ppermute | solution.py:217
  22.8 1.5 %all-to-all-done = bf16[16,16,96]{2,1,0:T(8,128)(2,1)S(1)} async-done(((bf16[16,16,96]{2,1,0:T(8,128)(2,1)}), bf16[16,16,96]{2,1,0:T(8,128)(2,1)S(1)}, u32[]{:S(2)}, u32[]{:S(2)}) %all-to-all-start) | async-done | bytes 49184 | tf_op jit(solution)/shard_map/all_to_all | solution.py:201
  24.3 0.0 copy-start.1
  24.3 0.2 shard_map.65
  24.5 0.0 copy-start
  24.5 17.7 %all_to_all.20.x_ref = bf16[16,96,256]{2,1,0:T(8,128)(2,1)S(1)} all-to-all(bf16[16,96,256]{2,1,0:T(8,128)(2,1)S(1)} %shard_map.65), channel_id=1, replica_groups={{30,0,2,4,6,8,10,12,14,16,18,20,22,24,26,28},{31,1,3,5,7,9,11,13,15,17,..., dimensions={0} | all-to-all | bytes 1572864 | tf_op jit(solution)/shard_map/all_to_all | solution.py:219
  42.2 0.0 collective-permute-done.got_ref
  42.2 0.0 copy-done.1
  42.2 0.0 copy-done
  42.2 1.1 %shard_map.67 = bf16[4,168,256]{2,1,0:T(8,128)(2,1)S(1)} custom-call(s32[1]{0:T(128)} %bitcast.2.core_ref, bf16[16,96,256]{2,1,0:T(8,128)(2,1)S(1)} %all_to_all.20.x_ref, bf16[168,3072]{1,0:T(8,128)(2,1)S(1)} %bitcast.11, bf16[168,3072]{1,0:T(8,128)(2,1)S(1)} %bitcast.13, bf16[3,168,1536]{2,1,0:T(8,128)(2,1)S(1)} %collective-permute-done.got_ref), custom_call_target="tpu_custom_call" | custom-call | flops 792723456 | bytes 4743168 | tf_op jit(solution)/shard_map/pallas_call | solution.py:44
  43.4 0.0 copy-start.2
  43.4 2.4 %all_gather.3.halves_ref = bf16[8,168,256]{2,1,0:T(8,128)(2,1)S(1)} all-gather(bf16[4,168,256]{2,1,0:T(8,128)(2,1)S(1)} %shard_map.67), channel_id=1, replica_groups={{0,1},{2,3},{4,5},{6,7},{8,9},{10,11},{12,13},{14,15},{16,17},{18,19},{..., dimensions={0}, use_global_device_ids=true | all-gather | bytes 1032192 | tf_op jit(solution)/shard_map/all_gather | solution.py:228
  45.8 0.0 copy-done.2
  45.8 1.0 %shard_map.68 = bf16[16,96,256]{2,1,0:T(8,128)(2,1)S(1)} custom-call(s32[1]{0:T(128)} %bitcast.2.core_ref, bf16[8,168,256]{2,1,0:T(8,128)(2,1)S(1)} %all_gather.3.halves_ref, bf16[168,3072]{1,0:T(8,128)(2,1)S(1)} %bitcast.15, bf16[3,168,1536]{2,1,0:T(8,128)(2,1)S(1)} %collective-permute-done.got_ref), custom_call_target="tpu_custom_call" | custom-call | flops 396361728 | bytes 4055040 | tf_op jit(solution)/shard_map/pallas_call | solution.py:44
  46.8 0.0 copy-start.3
  46.8 18.0 %all_to_all.21.pieces_ref = bf16[16,96,256]{2,1,0:T(8,128)(2,1)S(1)} all-to-all(bf16[16,96,256]{2,1,0:T(8,128)(2,1)S(1)} %shard_map.68), channel_id=1, replica_groups={{30,0,2,4,6,8,10,12,14,16,18,20,22,24,26,28},{31,1,3,5,7,9,11,13,15,17,..., dimensions={0} | all-to-all | bytes 1572864 | tf_op jit(solution)/shard_map/all_to_all | solution.py:237
  64.9 0.3 shard_map.69
  65.2 15.5 %all_to_all.22 = bf16[16,16,96]{2,1,0:T(8,128)(2,1)S(1)} all-to-all(bf16[16,16,96]{2,1,0:T(8,128)(2,1)S(1)} %bitcast.17), channel_id=1, replica_groups={{256,288,320,352,384,416,448,480,0,32,64,96,128,160,192,224},{257,289,3..., dimensions={0} | all-to-all | bytes 98304 | tf_op jit(solution)/shard_map/all_to_all | solution.py:239
  80.7 0.0 copy-done.3
  80.7 0.8 %shard_map.70 = bf16[32,96]{1,0:T(8,128)(2,1)} custom-call(f32[256,32]{1,0:T(8,128)S(1)} %copy-done.3, bf16[256,96]{1,0:T(8,128)(2,1)S(1)} %bitcast.16), custom_call_target="tpu_custom_call" | custom-call | bytes 88064 | tf_op jit(solution)/shard_map/pallas_call | solution.py:44
Async XLA Ops:
  1.7 22.5 %all-to-all-start = ((bf16[16,16,96]{2,1,0:T(8,128)(2,1)}), bf16[16,16,96]{2,1,0:T(8,128)(2,1)S(1)}, u32[]{:S(2)}, u32[]{:S(2)}) async-start(bf16[16,16,96]{2,1,0:T(8,128)(2,1)} %bitcast.19), calls=%async_computation | async-start | bytes 131072 | tf_op jit(solution)/shard_map/all_to_all | solution.py:201
  20.9 21.3 %collective-permute-start = (bf16[3,168,1536]{2,1,0:T(8,128)(2,1)}, bf16[3,168,1536]{2,1,0:T(8,128)(2,1)S(1)}, u32[]{:S(2)}, u32[]{:S(2)}) collective-permute-start(bf16[3,168,1536]{2,1,0:T(8,128)(2,1)} %shard_map.66), channel_id=1, source_target_pairs={{0,1},{1,0},{2,3},{3,2},{4,5},{5,4},{6,7},{7,6},{8,9},{9,8},{10,11... | collective-permute-start | bytes 4644872 | tf_op jit(solution)/shard_map/ppermute | solution.py:217
  24.3 17.9 %copy-start.1 = (bf16[1,168,3072]{2,1,0:T(8,128)(2,1)S(1)}, bf16[1,168,3072]{2,1,0:T(8,128)(2,1)}, u32[]{:S(2)}) copy-start(bf16[1,168,3072]{2,1,0:T(8,128)(2,1)} %param.10) | copy-start | bytes 3096580
  24.5 17.7 %copy-start = (bf16[1,168,3072]{2,1,0:T(8,128)(2,1)S(1)}, bf16[1,168,3072]{2,1,0:T(8,128)(2,1)}, u32[]{:S(2)}) copy-start(bf16[1,168,3072]{2,1,0:T(8,128)(2,1)} %param.9) | copy-start | bytes 3096580
  43.4 2.4 %copy-start.2 = (bf16[1,168,3072]{2,1,0:T(8,128)(2,1)S(1)}, bf16[1,168,3072]{2,1,0:T(8,128)(2,1)}, u32[]{:S(2)}) copy-start(bf16[1,168,3072]{2,1,0:T(8,128)(2,1)} %param.11) | copy-start | bytes 3096580
  46.8 33.9 %copy-start.3 = (f32[256,32]{1,0:T(8,128)S(1)}, f32[256,32]{1,0:T(8,128)}, u32[]{:S(2)}) copy-start(f32[256,32]{1,0:T(8,128)} %get-tuple-element.7.mix_ref) | copy-start | bytes 98308

commit v6 on v5

--- a/solution.py
+++ b/solution.py
@@ -12,7 +12,7 @@
 ANY = pl.BlockSpec(memory_space=pltpu.HBM)
 BF16 = jnp.bfloat16
 F32 = jnp.float32
-FIRST, LAST = 11, 8
+FIRST, LAST, CHIP = 11, 8, 10
 
 
 def dot(left, right, dims, precision=None):
@@ -32,7 +32,7 @@
 
 
 def chip_at(i, n):
-    return (i + n - 1) % n
+    return (i + CHIP * n // 16) % n
 
 
 def call(body, out, operands, flops=0, core=None, far=(), far_out=0, scratch=(), grant=20480):

time: 82.1 us -> 80.8 us (0.984)
  the two profiles are of different devices: /device:TPU:2 before, /device:TPU:4 now
where the time goes in v6:
time: 80.8 us; the launch traced here: 80.4 us
  blocking collectives  52.6 us (65%)
  starting transfers between devices  18.1 us (22%)
  Pallas kernels  8.21 us (10%)
  waiting for transfers between devices  1.42 us (2%)
    all_to_all x1, blocking collectives, local(): lax.all_to_all(copies, 'tensor', 0, 0, axis_index_groups=same_core, tiled...  17.4 us
    all_to_all x1, blocking collectives, local(): lax.all_to_all(part, 'tensor', 0, 0, axis_index_groups=same_core, tiled=T...  17.3 us
    all_to_all x1, starting transfers between devices, local(): lax.all_to_all(placed.reshape(experts, capacity, depth), 'expert', 0, 0,...  16.2 us
    all_to_all x1, blocking collectives, local(): lax.all_to_all(summed.reshape(experts, capacity, depth), 'expert', 0, 0,...  15.5 us
    pallas_call x7, Pallas kernels, call(): pl.pallas_call(body, out_shape=out, in_specs=specs, out_specs=tuple(out_s...  8.21 us
    all_gather x1, blocking collectives, local(): lax.all_gather(partial, 'tensor', axis=0, axis_index_groups=same_chip, ti...  2.43 us
    ppermute x1, starting transfers between devices, local(): got = lax.ppermute(send, 'tensor', [(i, i ^ 1) for i in range(2 * chips)])  1.92 us
  transfers between devices with their start and end apart: 2, of which 1 were waited for; matrix products, arithmetic and copies ran while one was open for 0% of the time, Pallas kernels for 4%

profile of v6, /device:TPU:4, one launch (start us, length us, event | category | flops | bytes accessed | tf_op | source)
XLA Modules:
  0.0 80.4 jit_solution(7793820438494009937)
XLA Ops:
  0.0 1.7 %shard_map.64 = (bf16[256,96]{1,0:T(8,128)(2,1)}, f32[256,32]{1,0:T(8,128)}) custom-call(bf16[32,96]{1,0:T(8,128)(2,1)} %tokens_far.1, s32[4,32]{1,0:T(4,128)} %bitcast.20, s32[4,32]{1,0:T(4,128)} %bitcast.21), custom_call_target="tpu_custom_call" | custom-call | bytes 81920 | tf_op jit(solution)/shard_map/pallas_call | solution.py:44
  1.7 16.2 %all-to-all-start = ((bf16[16,16,96]{2,1,0:T(8,128)(2,1)}), bf16[16,16,96]{2,1,0:T(8,128)(2,1)S(1)}, u32[]{:S(2)}, u32[]{:S(2)}) async-start(bf16[16,16,96]{2,1,0:T(8,128)(2,1)} %bitcast.19), calls=%async_computation | async-start | bytes 131072 | tf_op jit(solution)/shard_map/all_to_all | solution.py:201
  17.9 3.0 %shard_map.66 = bf16[3,168,1536]{2,1,0:T(8,128)(2,1)} custom-call(s32[1]{0:T(128)} %bitcast.2.core_ref, bf16[168,3072]{1,0:T(8,128)(2,1)} %bitcast.10, bf16[168,3072]{1,0:T(8,128)(2,1)} %bitcast.12, bf16[168,3072]{1,0:T(8,128)(2,1)} %bitcast.14, bf16[256,96]{1,0:T(8,128)(2,1)} %get-tuple-element.8._), custom_call_target="tpu_custom_call" | custom-call | flops 100000000 | bytes 1548288 | tf_op jit(solution)/shard_map/pallas_call | solution.py:44
  20.9 1.9 %collective-permute-start = (bf16[3,168,1536]{2,1,0:T(8,128)(2,1)}, bf16[3,168,1536]{2,1,0:T(8,128)(2,1)S(1)}, u32[]{:S(2)}, u32[]{:S(2)}) collective-permute-start(bf16[3,168,1536]{2,1,0:T(8,128)(2,1)} %shard_map.66), channel_id=1, source_target_pairs={{0,1},{1,0},{2,3},{3,2},{4,5},{5,4},{6,7},{7,6},{8,9},{9,8},{10,11... | collective-permute-start | bytes 4644872 | tf_op jit(solution)/shard_map/ppermute | solution.py:217
  22.8 1.4 %all-to-all-done = bf16[16,16,96]{2,1,0:T(8,128)(2,1)S(1)} async-done(((bf16[16,16,96]{2,1,0:T(8,128)(2,1)}), bf16[16,16,96]{2,1,0:T(8,128)(2,1)S(1)}, u32[]{:S(2)}, u32[]{:S(2)}) %all-to-all-start) | async-done | bytes 49184 | tf_op jit(solution)/shard_map/all_to_all | solution.py:201
  24.3 0.0 copy-start.1
  24.3 0.2 shard_map.65
  24.5 0.0 copy-start
  24.5 17.4 %all_to_all.20.x_ref = bf16[16,96,256]{2,1,0:T(8,128)(2,1)S(1)} all-to-all(bf16[16,96,256]{2,1,0:T(8,128)(2,1)S(1)} %shard_map.65), channel_id=1, replica_groups={{20,22,24,26,28,30,0,2,4,6,8,10,12,14,16,18},{21,23,25,27,29,31,1,3,5,7..., dimensions={0} | all-to-all | bytes 1572864 | tf_op jit(solution)/shard_map/all_to_all | solution.py:219
  41.9 0.0 collective-permute-done.got_ref
  41.9 0.0 copy-done.1
  41.9 0.0 copy-done
  41.9 1.1 %shard_map.67 = bf16[4,168,256]{2,1,0:T(8,128)(2,1)S(1)} custom-call(s32[1]{0:T(128)} %bitcast.2.core_ref, bf16[16,96,256]{2,1,0:T(8,128)(2,1)S(1)} %all_to_all.20.x_ref, bf16[168,3072]{1,0:T(8,128)(2,1)S(1)} %bitcast.11, bf16[168,3072]{1,0:T(8,128)(2,1)S(1)} %bitcast.13, bf16[3,168,1536]{2,1,0:T(8,128)(2,1)S(1)} %collective-permute-done.got_ref), custom_call_target="tpu_custom_call" | custom-call | flops 792723456 | bytes 4743168 | tf_op jit(solution)/shard_map/pallas_call | solution.py:44
  43.1 0.0 copy-start.2
  43.1 2.4 %all_gather.3.halves_ref = bf16[8,168,256]{2,1,0:T(8,128)(2,1)S(1)} all-gather(bf16[4,168,256]{2,1,0:T(8,128)(2,1)S(1)} %shard_map.67), channel_id=1, replica_groups={{0,1},{2,3},{4,5},{6,7},{8,9},{10,11},{12,13},{14,15},{16,17},{18,19},{..., dimensions={0}, use_global_device_ids=true | all-gather | bytes 1032192 | tf_op jit(solution)/shard_map/all_gather | solution.py:228
  45.5 0.0 copy-done.2
  45.5 1.0 %shard_map.68 = bf16[16,96,256]{2,1,0:T(8,128)(2,1)S(1)} custom-call(s32[1]{0:T(128)} %bitcast.2.core_ref, bf16[8,168,256]{2,1,0:T(8,128)(2,1)S(1)} %all_gather.3.halves_ref, bf16[168,3072]{1,0:T(8,128)(2,1)S(1)} %bitcast.15, bf16[3,168,1536]{2,1,0:T(8,128)(2,1)S(1)} %collective-permute-done.got_ref), custom_call_target="tpu_custom_call" | custom-call | flops 396361728 | bytes 4055040 | tf_op jit(solution)/shard_map/pallas_call | solution.py:44
  46.5 0.0 copy-start.3
  46.5 17.3 %all_to_all.21.pieces_ref = bf16[16,96,256]{2,1,0:T(8,128)(2,1)S(1)} all-to-all(bf16[16,96,256]{2,1,0:T(8,128)(2,1)S(1)} %shard_map.68), channel_id=1, replica_groups={{20,22,24,26,28,30,0,2,4,6,8,10,12,14,16,18},{21,23,25,27,29,31,1,3,5,7..., dimensions={0} | all-to-all | bytes 1572864 | tf_op jit(solution)/shard_map/all_to_all | solution.py:237
  63.8 0.3 shard_map.69
  64.1 15.5 %all_to_all.22 = bf16[16,16,96]{2,1,0:T(8,128)(2,1)S(1)} all-to-all(bf16[16,16,96]{2,1,0:T(8,128)(2,1)S(1)} %bitcast.17), channel_id=1, replica_groups={{256,288,320,352,384,416,448,480,0,32,64,96,128,160,192,224},{257,289,3..., dimensions={0} | all-to-all | bytes 98304 | tf_op jit(solution)/shard_map/all_to_all | solution.py:239
  79.6 0.0 copy-done.3
  79.6 0.8 %shard_map.70 = bf16[32,96]{1,0:T(8,128)(2,1)} custom-call(f32[256,32]{1,0:T(8,128)S(1)} %copy-done.3, bf16[256,96]{1,0:T(8,128)(2,1)S(1)} %bitcast.16), custom_call_target="tpu_custom_call" | custom-call | bytes 88064 | tf_op jit(solution)/shard_map/pallas_call | solution.py:44
Async XLA Ops:
  1.7 22.5 %all-to-all-start = ((bf16[16,16,96]{2,1,0:T(8,128)(2,1)}), bf16[16,16,96]{2,1,0:T(8,128)(2,1)S(1)}, u32[]{:S(2)}, u32[]{:S(2)}) async-start(bf16[16,16,96]{2,1,0:T(8,128)(2,1)} %bitcast.19), calls=%async_computation | async-start | bytes 131072 | tf_op jit(solution)/shard_map/all_to_all | solution.py:201
  20.9 21.0 %collective-permute-start = (bf16[3,168,1536]{2,1,0:T(8,128)(2,1)}, bf16[3,168,1536]{2,1,0:T(8,128)(2,1)S(1)}, u32[]{:S(2)}, u32[]{:S(2)}) collective-permute-start(bf16[3,168,1536]{2,1,0:T(8,128)(2,1)} %shard_map.66), channel_id=1, source_target_pairs={{0,1},{1,0},{2,3},{3,2},{4,5},{5,4},{6,7},{7,6},{8,9},{9,8},{10,11... | collective-permute-start | bytes 4644872 | tf_op jit(solution)/shard_map/ppermute | solution.py:217
  24.3 17.6 %copy-start.1 = (bf16[1,168,3072]{2,1,0:T(8,128)(2,1)S(1)}, bf16[1,168,3072]{2,1,0:T(8,128)(2,1)}, u32[]{:S(2)}) copy-start(bf16[1,168,3072]{2,1,0:T(8,128)(2,1)} %param.10) | copy-start | bytes 3096580
  24.5 17.4 %copy-start = (bf16[1,168,3072]{2,1,0:T(8,128)(2,1)S(1)}, bf16[1,168,3072]{2,1,0:T(8,128)(2,1)}, u32[]{:S(2)}) copy-start(bf16[1,168,3072]{2,1,0:T(8,128)(2,1)} %param.9) | copy-start | bytes 3096580
  43.1 2.4 %copy-start.2 = (bf16[1,168,3072]{2,1,0:T(8,128)(2,1)S(1)}, bf16[1,168,3072]{2,1,0:T(8,128)(2,1)}, u32[]{:S(2)}) copy-start(bf16[1,168,3072]{2,1,0:T(8,128)(2,1)} %param.11) | copy-start | bytes 3096580
  46.5 33.1 %copy-start.3 = (f32[256,32]{1,0:T(8,128)S(1)}, f32[256,32]{1,0:T(8,128)}, u32[]{:S(2)}) copy-start(f32[256,32]{1,0:T(8,128)} %get-tuple-element.7.mix_ref) | copy-start | bytes 98308

commit v7 on v6

--- a/solution.py
+++ b/solution.py
@@ -12,7 +12,7 @@
 ANY = pl.BlockSpec(memory_space=pltpu.HBM)
 BF16 = jnp.bfloat16
 F32 = jnp.float32
-FIRST, LAST, CHIP = 11, 8, 10
+FIRST, LAST, CHIP, EARLY = 10, 9, 10, 5
 
 
 def dot(left, right, dims, precision=None):
@@ -35,7 +35,7 @@
     return (i + CHIP * n // 16) % n
 
 
-def call(body, out, operands, flops=0, core=None, far=(), far_out=0, scratch=(), grant=20480):
+def call(body, out, operands, flops=0, core=None, far=(), far_out=0, aliases={}, scratch=(), grant=20480):
     scalar = () if core is None else (core,)
     specs = [pl.BlockSpec(memory_space=pltpu.SMEM)] * len(scalar) + [VMEM] * len(operands) + [ANY] * len(far)
     outs = jax.tree.leaves(out)
@@ -46,6 +46,7 @@
         out_shape=out,
         in_specs=specs,
         out_specs=tuple(out_specs) if isinstance(out, tuple) else out_specs[0],
+        input_output_aliases=aliases,
         scratch_shapes=list(scratch),
         compiler_params=pltpu.CompilerParams(vmem_limit_bytes=grant * 2**10),
         cost_estimate=pl.CostEstimate(flops=flops, bytes_accessed=moved, transcendentals=0),
@@ -59,9 +60,45 @@
     return copies
 
 
-def place_kernel(capacity, first, shift, tokens_far, routes_far, weight_far, placed_ref, mix_ref, tokens_ref, routes_ref, weight_ref, sems):
+def pick_columns(depth, core, fars, send_far, own_far, weights_ref, send_ref, own_ref, out_sems, sems):
+    n = weights_ref.shape[2] // (2 * depth)
+    thin = 4 * depth
+    stores = []
+    for k, load_far in enumerate(fars):
+        pltpu.make_async_copy(load_far, weights_ref.at[k], sems.at[k]).wait()
+        for which in range(2):
+
+            @pl.when(core == which)
+            def _():
+                for ref, part in ((send_ref, 1 - which), (own_ref, which)):
+                    for g in range(n // 4):
+                        starts = [(2 * chip_at(4 * g + i, n) + part) * depth for i in range(4)]
+                        pieces = [weights_ref[k, :, start : start + depth] for start in starts]
+                        ref[k, :, g * thin : (g + 1) * thin] = jnp.concatenate(pieces, axis=1)
+
+        for i, (ref, far) in enumerate(((send_ref, send_far), (own_ref, own_far))):
+            store = pltpu.make_async_copy(ref.at[k], far.at[k], out_sems.at[i, k])
+            store.start()
+            stores.append(store)
+    for store in stores:
+        store.wait()
+
+
+def place_kernel(
+    depth, capacity, first, shift, where_ref, tokens_far, routes_far, weight_far, gate_far, up_far, down_far,
+    placed_ref, mix_ref, send_far, own_far,
+    tokens_ref, routes_ref, weight_ref, weights_ref, send_ref, own_ref, sems, weight_sems, out_sems,
+):
     pairs = ((tokens_far, tokens_ref), (routes_far, routes_ref), (weight_far, weight_ref))
-    for copy in fetch(pairs, sems):
+    copies = fetch(pairs, sems)
+    fars = (gate_far, up_far, down_far)
+    early = where_ref[0] < 2 * EARLY
+
+    @pl.when(early)
+    def _():
+        fetch([(far, weights_ref.at[k]) for k, far in enumerate(fars)], weight_sems)
+
+    for copy in copies:
         copy.wait()
     top, rows = routes_ref.shape
     slots = placed_ref.shape[0]
@@ -84,6 +121,10 @@
     dispatch = jnp.where(here, 1.0, 0.0).astype(BF16)
     placed_ref[...] = dot(dispatch, tokens_ref[...], ((1,), (0,))).astype(BF16)
 
+    @pl.when(early)
+    def _():
+        pick_columns(depth, where_ref[0] % 2, fars, send_far, own_far, weights_ref, send_ref, own_ref, out_sems, weight_sems)
+
 
 def turn_kernel(arrived_ref, copies_ref):
     n, depth, _ = copies_ref.shape
@@ -92,59 +133,39 @@
         copies_ref[i] = turned
 
 
-def pick_kernel(depth, core_ref, gate_far, up_far, down_far, _, send_far, weights_ref, send_ref, sems, out_sems):
-    loads = fetch([(far, weights_ref.at[k]) for k, far in enumerate((gate_far, up_far, down_far))], sems)
-    n = weights_ref.shape[2] // (2 * depth)
-    thin = 4 * depth
-    stores = []
-    for k, load in enumerate(loads):
-        load.wait()
-        for which in range(2):
-
-            @pl.when(core_ref[0] != which)
-            def _():
-                for g in range(n // 4):
-                    starts = [(2 * chip_at(4 * g + i, n) + which) * depth for i in range(4)]
-                    pieces = [weights_ref[k, :, start : start + depth] for start in starts]
-                    send_ref[k, :, g * thin : (g + 1) * thin] = jnp.concatenate(pieces, axis=1)
-
-        store = pltpu.make_async_copy(send_ref.at[k], send_far.at[k], out_sems.at[k])
-        store.start()
-        stores.append(store)
-    for store in stores:
-        store.wait()
-
-
-def rise_kernel(core_ref, x_ref, gate_ref, up_ref, got_ref, out_ref, spread_ref):
-    own, other = core_ref[0], 1 - core_ref[0]
-    n, depth, _ = x_ref.shape
-    for i in range(n):
-        chip = chip_at(i, n)
-        spread_ref[pl.ds(pl.multiple_of((2 * chip + own) * depth, depth), depth)] = x_ref[i]
-        spread_ref[pl.ds(pl.multiple_of((2 * chip + other) * depth, depth), depth)] = jnp.zeros_like(x_ref[i])
-    x = x_ref[...].reshape(n * depth, x_ref.shape[2])
-    for k, ref in enumerate((gate_ref, up_ref)):
-        out_ref[2 * own + k] = dot(ref[...], spread_ref[...], ((1,), (0,))).astype(BF16)
-        out_ref[2 * other + k] = dot(got_ref[k], x, ((1,), (0,))).astype(BF16)
-
-
-def fall_kernel(core_ref, halves_ref, down_ref, got_ref, out_ref, part_ref):
-    own, other = core_ref[0], 1 - core_ref[0]
+def pick_kernel(
+    depth, where_ref, gate_far, up_far, down_far, _, __, send_far, own_far, weights_ref, send_ref, own_ref, sems, out_sems
+):
+    fars = (gate_far, up_far, down_far)
+
+    @pl.when(where_ref[0] >= 2 * EARLY)
+    def _():
+        fetch([(far, weights_ref.at[k]) for k, far in enumerate(fars)], sems)
+        pick_columns(depth, where_ref[0] % 2, fars, send_far, own_far, weights_ref, send_ref, own_ref, out_sems, sems)
+
+
+def rise_kernel(core_ref, x_ref, own_ref, got_ref, out_ref):
+    n, depth, slots = x_ref.shape
+    x = x_ref[...].reshape(n * depth, slots)
+    for ref, which in ((own_ref, core_ref[0]), (got_ref, 1 - core_ref[0])):
+        for k in range(2):
+            out_ref[2 * which + k] = dot(ref[k], x, ((1,), (0,))).astype(BF16)
+
+
+def fall_kernel(core_ref, halves_ref, own_ref, got_ref, out_ref):
     n, depth, _ = out_ref.shape
     hidden = []
-    for u in (own, other):
+    for u in (core_ref[0], 1 - core_ref[0]):
         gate = halves_ref[2 * u].astype(F32) + halves_ref[4 + 2 * u].astype(F32)
         up = halves_ref[2 * u + 1].astype(F32) + halves_ref[5 + 2 * u].astype(F32)
         hidden.append((gate / (1.0 + jnp.exp(-gate)) * up).astype(BF16))
-    part_ref[...] = dot(down_ref[...], hidden[0], ((0,), (0,)))
     group = 4
     for g in range(n // group):
         columns = slice(g * group * depth, (g + 1) * group * depth)
-        rest = dot(got_ref[2, :, columns], hidden[1], ((0,), (0,)))
+        part = dot(own_ref[2, :, columns], hidden[0], ((0,), (0,)))
+        part += dot(got_ref[2, :, columns], hidden[1], ((0,), (0,)))
         for j in range(group):
-            i = g * group + j
-            first = part_ref[pl.ds(pl.multiple_of((2 * chip_at(i, n) + own) * depth, depth), depth)]
-            out_ref[i] = (first + rest[j * depth : (j + 1) * depth]).astype(BF16)
+            out_ref[g * group + j] = part[j * depth : (j + 1) * depth].astype(BF16)
 
 
 def sum_kernel(shift, pieces_ref, out_ref):
@@ -181,37 +202,47 @@
     same_core = [[2 * chip_at(i, chips) + c for i in range(chips)] for c in range(2)]
     same_chip = [[2 * i, 2 * i + 1] for i in range(chips)]
     core = (lax.axis_index("tensor") % 2).astype(jnp.int32).reshape(1)
+    where = (lax.axis_index("expert") * 2 + lax.axis_index("tensor") % 2).astype(jnp.int32).reshape(1)
 
     def shape(*dims, dtype=BF16):
         return jax.ShapeDtypeStruct(dims, dtype)
 
-    placed, mix = call(
-        functools.partial(place_kernel, capacity, first, shift),
-        (shape(slots, depth), shape(slots, rows, dtype=F32)),
+    weights = (w_gate[0], w_up[0], w_down[0])
+    thirds = shape(3, units, half)
+    picking = (
+        pltpu.VMEM((3, units, width), BF16),
+        pltpu.VMEM(thirds.shape, BF16),
+        pltpu.VMEM(thirds.shape, BF16),
+    )
+    placed, mix, send, own = call(
+        functools.partial(place_kernel, depth, capacity, first, shift),
+        (shape(slots, depth), shape(slots, rows, dtype=F32), thirds, thirds),
         (),
-        far=(tokens, routes.T, route_weight.T),
+        core=where,
+        far=(tokens, routes.T, route_weight.T, *weights),
+        far_out=2,
         scratch=(
             pltpu.VMEM(tokens.shape, tokens.dtype),
             pltpu.VMEM(routes.shape[::-1], routes.dtype),
             pltpu.VMEM(routes.shape[::-1], route_weight.dtype),
-            pltpu.SemaphoreType.DMA((3,)),
+            *picking,
+            *[pltpu.SemaphoreType.DMA((3,))] * 2,
+            pltpu.SemaphoreType.DMA((2, 3)),
         ),
         grant=65536,
     )
     arrived = lax.all_to_all(placed.reshape(experts, capacity, depth), "expert", 0, 0, axis_index_groups=order_out, tiled=True)
 
-    weights = (w_gate[0], w_up[0], w_down[0])
-    thirds = shape(3, units, half)
-    whole_ref, third_ref = pltpu.VMEM((3, units, width), BF16), pltpu.VMEM(thirds.shape, BF16)
-    send = call(
+    send, own = call(
         functools.partial(pick_kernel, depth),
-        thirds,
+        (thirds, thirds),
         (),
         flops=10**8,
-        core=core,
-        far=(*weights, placed),
-        far_out=1,
-        scratch=(whole_ref, third_ref, pltpu.SemaphoreType.DMA((3,)), pltpu.SemaphoreType.DMA((3,))),
+        core=where,
+        far=(*weights, send, own),
+        far_out=2,
+        aliases={4: 0, 5: 1},
+        scratch=(*picking, pltpu.SemaphoreType.DMA((3,)), pltpu.SemaphoreType.DMA((2, 3))),
         grant=65024,
     )
     got = lax.ppermute(send, "tensor", [(i, i ^ 1) for i in range(2 * chips)])
@@ -220,19 +251,17 @@
     partial = call(
         rise_kernel,
         shape(4, units, slots),
-        (x, *weights[:2], got),
-        flops=2 * 6 * units * half * slots,
+        (x, own, got),
+        flops=2 * 4 * units * half * slots,
         core=core,
-        scratch=(pltpu.VMEM((width, slots), BF16),),
     )
     halves = lax.all_gather(partial, "tensor", axis=0, axis_index_groups=same_chip, tiled=True)
     part = call(
         fall_kernel,
         shape(chips, depth, slots),
-        (halves, weights[2], got),
-        flops=2 * 3 * units * half * slots,
+        (halves, own, got),
+        flops=2 * 2 * units * half * slots,
         core=core,
-        scratch=(pltpu.VMEM((width, slots), F32),),
     )
     pieces = lax.all_to_all(part, "tensor", 0, 0, axis_index_groups=same_core, tiled=True)
     summed = call(functools.partial(sum_kernel, shift), shape(slots, depth), (pieces,))

time: 80.8 us -> 79.8 us (0.988)
  the two profiles are of different devices: /device:TPU:4 before, /device:TPU:2 now
where the time goes in v7:
time: 79.8 us; the launch traced here: 79.2 us
  blocking collectives  52 us (65%)
  starting transfers between devices  15.8 us (20%)
  Pallas kernels  7.86 us (10%)
  waiting for transfers between devices  3.46 us (4%)
    all_to_all x1, blocking collectives, local(): lax.all_to_all(part, 'tensor', 0, 0, axis_index_groups=same_core, tiled=T...  17.2 us
    all_to_all x1, blocking collectives, local(): lax.all_to_all(copies, 'tensor', 0, 0, axis_index_groups=same_core, tiled...  16.8 us
    all_to_all x1, blocking collectives, local(): lax.all_to_all(summed.reshape(experts, capacity, depth), 'expert', 0, 0,...  15.7 us
    all_to_all x1, starting transfers between devices, local(): lax.all_to_all(placed.reshape(experts, capacity, depth), 'expert', 0, 0,...  13.9 us
    pallas_call x7, Pallas kernels, call(): pl.pallas_call(body, out_shape=out, in_specs=specs, out_specs=tuple(out_s...  7.86 us
    all_to_all x1, waiting for transfers between devices, local(): lax.all_to_all(placed.reshape(experts, capacity, depth), 'expert', 0, 0,...  3.45 us
    all_gather x1, blocking collectives, local(): lax.all_gather(partial, 'tensor', axis=0, axis_index_groups=same_chip, ti...  2.3 us
    ppermute x1, starting transfers between devices, local(): got = lax.ppermute(send, 'tensor', [(i, i ^ 1) for i in range(2 * chips)])  1.92 us
  transfers between devices with their start and end apart: 2, of which 1 were waited for; matrix products, arithmetic and copies ran while one was open for 0% of the time, Pallas kernels for 0%

profile of v7, /device:TPU:2, one launch (start us, length us, event | category | flops | bytes accessed | tf_op | source)
XLA Modules:
  0.0 79.2 jit_solution(15692758466649509554)
XLA Ops:
  0.0 5.1 %shard_map.64 = (bf16[256,96]{1,0:T(8,128)(2,1)}, f32[256,32]{1,0:T(8,128)}, bf16[3,168,1536]{2,1,0:T(8,128)(2,1)}, bf16[3,168,1536]{2,1,0:T(8,128)(2,1)}) custom-call(s32[1]{0:T(128)} %bitcast.where_ref, bf16[32,96]{1,0:T(8,128)(2,1)} %tokens_far.1, s32[4,32]{1,0:T(4,128)} %bitcast.21, s32[4,32]{1,0:T(4,128)} %bitcast.22, bf16[168,3072]{1,0:T(8,128)(2,1)} %bitcast.14, ...), custom_call_target="tpu_custom_call" | custom-call | bytes 3178496 | tf_op jit(solution)/shard_map/pallas_call | solution.py:44
  5.1 13.9 %all-to-all-start = ((bf16[16,16,96]{2,1,0:T(8,128)(2,1)}), bf16[16,16,96]{2,1,0:T(8,128)(2,1)S(1)}, u32[]{:S(2)}, u32[]{:S(2)}) async-start(bf16[16,16,96]{2,1,0:T(8,128)(2,1)} %bitcast.20), calls=%async_computation | async-start | bytes 131072 | tf_op jit(solution)/shard_map/all_to_all | solution.py:234
  18.9 0.1 shard_map.66
  19.0 1.9 %collective-permute-start = (bf16[3,168,1536]{2,1,0:T(8,128)(2,1)}, bf16[3,168,1536]{2,1,0:T(8,128)(2,1)S(1)}, u32[]{:S(2)}, u32[]{:S(2)}) collective-permute-start(bf16[3,168,1536]{2,1,0:T(8,128)(2,1)} %get-tuple-element.16), channel_id=1, source_target_pairs={{0,1},{1,0},{2,3},{3,2},{4,5},{5,4},{6,7},{7,6},{8,9},{9,8},{10,11... | collective-permute-start | bytes 4644872 | tf_op jit(solution)/shard_map/ppermute | solution.py:248
  21.0 3.5 %all-to-all-done = bf16[16,16,96]{2,1,0:T(8,128)(2,1)S(1)} async-done(((bf16[16,16,96]{2,1,0:T(8,128)(2,1)}), bf16[16,16,96]{2,1,0:T(8,128)(2,1)S(1)}, u32[]{:S(2)}, u32[]{:S(2)}) %all-to-all-start) | async-done | bytes 49184 | tf_op jit(solution)/shard_map/all_to_all | solution.py:234
  24.4 0.2 shard_map.65
  24.6 0.0 copy-start
  24.6 16.8 %all_to_all.20.x_ref = bf16[16,96,256]{2,1,0:T(8,128)(2,1)S(1)} all-to-all(bf16[16,96,256]{2,1,0:T(8,128)(2,1)S(1)} %shard_map.65), channel_id=1, replica_groups={{20,22,24,26,28,30,0,2,4,6,8,10,12,14,16,18},{21,23,25,27,29,31,1,3,5,7..., dimensions={0} | all-to-all | bytes 1572864 | tf_op jit(solution)/shard_map/all_to_all | solution.py:250
  41.4 0.0 collective-permute-done.got_ref
  41.4 0.0 copy-done
  41.4 0.7 shard_map.67
  42.1 2.3 %all_gather.3.halves_ref = bf16[8,168,256]{2,1,0:T(8,128)(2,1)S(1)} all-gather(bf16[4,168,256]{2,1,0:T(8,128)(2,1)S(1)} %shard_map.67), channel_id=1, replica_groups={{0,1},{2,3},{4,5},{6,7},{8,9},{10,11},{12,13},{14,15},{16,17},{18,19},{..., dimensions={0}, use_global_device_ids=true | all-gather | bytes 1032192 | tf_op jit(solution)/shard_map/all_gather | solution.py:258
  44.4 0.7 shard_map.68
  45.1 0.0 copy-start.1
  45.1 17.2 %all_to_all.21.pieces_ref = bf16[16,96,256]{2,1,0:T(8,128)(2,1)S(1)} all-to-all(bf16[16,96,256]{2,1,0:T(8,128)(2,1)S(1)} %shard_map.68), channel_id=1, replica_groups={{20,22,24,26,28,30,0,2,4,6,8,10,12,14,16,18},{21,23,25,27,29,31,1,3,5,7..., dimensions={0} | all-to-all | bytes 1572864 | tf_op jit(solution)/shard_map/all_to_all | solution.py:266
  62.4 0.3 shard_map.69
  62.7 15.7 %all_to_all.22 = bf16[16,16,96]{2,1,0:T(8,128)(2,1)S(1)} all-to-all(bf16[16,16,96]{2,1,0:T(8,128)(2,1)S(1)} %bitcast.12), channel_id=1, replica_groups={{288,320,352,384,416,448,480,0,32,64,96,128,160,192,224,256},{289,321,3..., dimensions={0} | all-to-all | bytes 98304 | tf_op jit(solution)/shard_map/all_to_all | solution.py:268
  78.4 0.0 copy-done.1
  78.4 0.8 %shard_map.70 = bf16[32,96]{1,0:T(8,128)(2,1)} custom-call(f32[256,32]{1,0:T(8,128)S(1)} %copy-done.1, bf16[256,96]{1,0:T(8,128)(2,1)S(1)} %bitcast.11), custom_call_target="tpu_custom_call" | custom-call | bytes 88064 | tf_op jit(solution)/shard_map/pallas_call | solution.py:44
Async XLA Ops:
  5.1 19.3 %all-to-all-start = ((bf16[16,16,96]{2,1,0:T(8,128)(2,1)}), bf16[16,16,96]{2,1,0:T(8,128)(2,1)S(1)}, u32[]{:S(2)}, u32[]{:S(2)}) async-start(bf16[16,16,96]{2,1,0:T(8,128)(2,1)} %bitcast.20), calls=%async_computation | async-start | bytes 131072 | tf_op jit(solution)/shard_map/all_to_all | solution.py:234
  19.0 22.4 %collective-permute-start = (bf16[3,168,1536]{2,1,0:T(8,128)(2,1)}, bf16[3,168,1536]{2,1,0:T(8,128)(2,1)S(1)}, u32[]{:S(2)}, u32[]{:S(2)}) collective-permute-start(bf16[3,168,1536]{2,1,0:T(8,128)(2,1)} %get-tuple-element.16), channel_id=1, source_target_pairs={{0,1},{1,0},{2,3},{3,2},{4,5},{5,4},{6,7},{7,6},{8,9},{9,8},{10,11... | collective-permute-start | bytes 4644872 | tf_op jit(solution)/shard_map/ppermute | solution.py:248
  24.6 16.8 %copy-start = (bf16[3,168,1536]{2,1,0:T(8,128)(2,1)S(1)}, bf16[3,168,1536]{2,1,0:T(8,128)(2,1)}, u32[]{:S(2)}) copy-start(bf16[3,168,1536]{2,1,0:T(8,128)(2,1)} %get-tuple-element.15.own_ref) | copy-start | bytes 4644868
  45.1 33.3 %copy-start.1 = (f32[256,32]{1,0:T(8,128)S(1)}, f32[256,32]{1,0:T(8,128)}, u32[]{:S(2)}) copy-start(f32[256,32]{1,0:T(8,128)} %get-tuple-element.11.mix_ref) | copy-start | bytes 98308

commit v8 on v7

--- a/solution.py
+++ b/solution.py
@@ -12,7 +12,7 @@
 ANY = pl.BlockSpec(memory_space=pltpu.HBM)
 BF16 = jnp.bfloat16
 F32 = jnp.float32
-FIRST, LAST, CHIP, EARLY = 10, 9, 10, 5
+FIRST, LAST, CHIP, EARLY = 10, 9, 10, 4
 
 
 def dot(left, right, dims, precision=None):

time: 79.8 us -> 79.8 us (level)
  the two profiles are of different devices: /device:TPU:2 before, /device:TPU:4 now
where the time goes in v8:
time: 79.8 us; the launch traced here: 79.4 us
  blocking collectives  52.2 us (65%)
  starting transfers between devices  15.8 us (20%)
  Pallas kernels  7.88 us (10%)
  waiting for transfers between devices  3.46 us (4%)
    all_to_all x1, blocking collectives, local(): lax.all_to_all(part, 'tensor', 0, 0, axis_index_groups=same_core, tiled=T...  17.2 us
    all_to_all x1, blocking collectives, local(): lax.all_to_all(copies, 'tensor', 0, 0, axis_index_groups=same_core, tiled...  17 us
    all_to_all x1, blocking collectives, local(): lax.all_to_all(summed.reshape(experts, capacity, depth), 'expert', 0, 0,...  15.7 us
    all_to_all x1, starting transfers between devices, local(): lax.all_to_all(placed.reshape(experts, capacity, depth), 'expert', 0, 0,...  13.9 us
    pallas_call x7, Pallas kernels, call(): pl.pallas_call(body, out_shape=out, in_specs=specs, out_specs=tuple(out_s...  7.88 us
    all_to_all x1, waiting for transfers between devices, local(): lax.all_to_all(placed.reshape(experts, capacity, depth), 'expert', 0, 0,...  3.45 us
    all_gather x1, blocking collectives, local(): lax.all_gather(partial, 'tensor', axis=0, axis_index_groups=same_chip, ti...  2.3 us
    ppermute x1, starting transfers between devices, local(): got = lax.ppermute(send, 'tensor', [(i, i ^ 1) for i in range(2 * chips)])  1.92 us
  transfers between devices with their start and end apart: 2, of which 1 were waited for; matrix products, arithmetic and copies ran while one was open for 0% of the time, Pallas kernels for 0%

profile of v8, /device:TPU:4, one launch (start us, length us, event | category | flops | bytes accessed | tf_op | source)
XLA Modules:
  0.0 79.4 jit_solution(18403922563075469220)
XLA Ops:
  0.0 5.1 %shard_map.64 = (bf16[256,96]{1,0:T(8,128)(2,1)}, f32[256,32]{1,0:T(8,128)}, bf16[3,168,1536]{2,1,0:T(8,128)(2,1)}, bf16[3,168,1536]{2,1,0:T(8,128)(2,1)}) custom-call(s32[1]{0:T(128)} %bitcast.where_ref, bf16[32,96]{1,0:T(8,128)(2,1)} %tokens_far.1, s32[4,32]{1,0:T(4,128)} %bitcast.21, s32[4,32]{1,0:T(4,128)} %bitcast.22, bf16[168,3072]{1,0:T(8,128)(2,1)} %bitcast.14, ...), custom_call_target="tpu_custom_call" | custom-call | bytes 3178496 | tf_op jit(solution)/shard_map/pallas_call | solution.py:44
  5.1 13.9 %all-to-all-start = ((bf16[16,16,96]{2,1,0:T(8,128)(2,1)}), bf16[16,16,96]{2,1,0:T(8,128)(2,1)S(1)}, u32[]{:S(2)}, u32[]{:S(2)}) async-start(bf16[16,16,96]{2,1,0:T(8,128)(2,1)} %bitcast.20), calls=%async_computation | async-start | bytes 131072 | tf_op jit(solution)/shard_map/all_to_all | solution.py:234
  18.9 0.1 shard_map.66
  19.0 1.9 %collective-permute-start = (bf16[3,168,1536]{2,1,0:T(8,128)(2,1)}, bf16[3,168,1536]{2,1,0:T(8,128)(2,1)S(1)}, u32[]{:S(2)}, u32[]{:S(2)}) collective-permute-start(bf16[3,168,1536]{2,1,0:T(8,128)(2,1)} %get-tuple-element.16), channel_id=1, source_target_pairs={{0,1},{1,0},{2,3},{3,2},{4,5},{5,4},{6,7},{7,6},{8,9},{9,8},{10,11... | collective-permute-start | bytes 4644872 | tf_op jit(solution)/shard_map/ppermute | solution.py:248
  21.0 3.5 %all-to-all-done = bf16[16,16,96]{2,1,0:T(8,128)(2,1)S(1)} async-done(((bf16[16,16,96]{2,1,0:T(8,128)(2,1)}), bf16[16,16,96]{2,1,0:T(8,128)(2,1)S(1)}, u32[]{:S(2)}, u32[]{:S(2)}) %all-to-all-start) | async-done | bytes 49184 | tf_op jit(solution)/shard_map/all_to_all | solution.py:234
  24.4 0.2 shard_map.65
  24.6 0.0 copy-start
  24.6 17.0 %all_to_all.20.x_ref = bf16[16,96,256]{2,1,0:T(8,128)(2,1)S(1)} all-to-all(bf16[16,96,256]{2,1,0:T(8,128)(2,1)S(1)} %shard_map.65), channel_id=1, replica_groups={{20,22,24,26,28,30,0,2,4,6,8,10,12,14,16,18},{21,23,25,27,29,31,1,3,5,7..., dimensions={0} | all-to-all | bytes 1572864 | tf_op jit(solution)/shard_map/all_to_all | solution.py:250
  41.6 0.0 collective-permute-done.got_ref
  41.6 0.0 copy-done
  41.6 0.7 shard_map.67
  42.4 2.3 %all_gather.3.halves_ref = bf16[8,168,256]{2,1,0:T(8,128)(2,1)S(1)} all-gather(bf16[4,168,256]{2,1,0:T(8,128)(2,1)S(1)} %shard_map.67), channel_id=1, replica_groups={{0,1},{2,3},{4,5},{6,7},{8,9},{10,11},{12,13},{14,15},{16,17},{18,19},{..., dimensions={0}, use_global_device_ids=true | all-gather | bytes 1032192 | tf_op jit(solution)/shard_map/all_gather | solution.py:258
  44.7 0.7 shard_map.68
  45.3 0.0 copy-start.1
  45.3 17.2 %all_to_all.21.pieces_ref = bf16[16,96,256]{2,1,0:T(8,128)(2,1)S(1)} all-to-all(bf16[16,96,256]{2,1,0:T(8,128)(2,1)S(1)} %shard_map.68), channel_id=1, replica_groups={{20,22,24,26,28,30,0,2,4,6,8,10,12,14,16,18},{21,23,25,27,29,31,1,3,5,7..., dimensions={0} | all-to-all | bytes 1572864 | tf_op jit(solution)/shard_map/all_to_all | solution.py:266
  62.6 0.3 shard_map.69
  62.9 15.7 %all_to_all.22 = bf16[16,16,96]{2,1,0:T(8,128)(2,1)S(1)} all-to-all(bf16[16,16,96]{2,1,0:T(8,128)(2,1)S(1)} %bitcast.12), channel_id=1, replica_groups={{288,320,352,384,416,448,480,0,32,64,96,128,160,192,224,256},{289,321,3..., dimensions={0} | all-to-all | bytes 98304 | tf_op jit(solution)/shard_map/all_to_all | solution.py:268
  78.6 0.0 copy-done.1
  78.6 0.8 %shard_map.70 = bf16[32,96]{1,0:T(8,128)(2,1)} custom-call(f32[256,32]{1,0:T(8,128)S(1)} %copy-done.1, bf16[256,96]{1,0:T(8,128)(2,1)S(1)} %bitcast.11), custom_call_target="tpu_custom_call" | custom-call | bytes 88064 | tf_op jit(solution)/shard_map/pallas_call | solution.py:44
Async XLA Ops:
  5.1 19.3 %all-to-all-start = ((bf16[16,16,96]{2,1,0:T(8,128)(2,1)}), bf16[16,16,96]{2,1,0:T(8,128)(2,1)S(1)}, u32[]{:S(2)}, u32[]{:S(2)}) async-start(bf16[16,16,96]{2,1,0:T(8,128)(2,1)} %bitcast.20), calls=%async_computation | async-start | bytes 131072 | tf_op jit(solution)/shard_map/all_to_all | solution.py:234
  19.0 22.6 %collective-permute-start = (bf16[3,168,1536]{2,1,0:T(8,128)(2,1)}, bf16[3,168,1536]{2,1,0:T(8,128)(2,1)S(1)}, u32[]{:S(2)}, u32[]{:S(2)}) collective-permute-start(bf16[3,168,1536]{2,1,0:T(8,128)(2,1)} %get-tuple-element.16), channel_id=1, source_target_pairs={{0,1},{1,0},{2,3},{3,2},{4,5},{5,4},{6,7},{7,6},{8,9},{9,8},{10,11... | collective-permute-start | bytes 4644872 | tf_op jit(solution)/shard_map/ppermute | solution.py:248
  24.6 17.0 %copy-start = (bf16[3,168,1536]{2,1,0:T(8,128)(2,1)S(1)}, bf16[3,168,1536]{2,1,0:T(8,128)(2,1)}, u32[]{:S(2)}) copy-start(bf16[3,168,1536]{2,1,0:T(8,128)(2,1)} %get-tuple-element.15.own_ref) | copy-start | bytes 4644868
  45.3 33.3 %copy-start.1 = (f32[256,32]{1,0:T(8,128)S(1)}, f32[256,32]{1,0:T(8,128)}, u32[]{:S(2)}) copy-start(f32[256,32]{1,0:T(8,128)} %get-tuple-element.11.mix_ref) | copy-start | bytes 98308
